TPU v7x, 256 devices: a whole 4x4x8 slice. The times are simulated.
256 devices in a mesh: row: 16 (over z_lo, y), col: 16 (over x, z_hi, core).
Axes of the slice: x: 4, y: 4, z: 8 (z_hi: 2, z_lo: 4; z = z_hi * 4 + z_lo), core: 2. Of those that a mesh axis runs over, the one named last changes fastest.
Arguments:
- points: bfloat16 [4096, 64], P('row'), may hold values from -1.5 to 1.5
- pivots: int32 [512], replicated, may hold values from 0 to 266239, as said below
- right_values: float32 [4096, 16], P('row'), may hold values from -6 to 6
- right_derivs: float32 [4096, 1024], P('row'), may hold values from -6 to 6
Outputs:
- solution_values: float32 [4096, 16], P(('row', 'col'))
- solution_derivs: float32 [4096, 1024], P(('row', 'col'))
- residual_values: float32 [4096, 16], P(('row', 'col'))
- residual_derivs: float32 [4096, 1024], P(('row', 'col'))
Inputs may be any that keep to these rules, and one draw needn't show every extreme that they name: `pivots`: distinct unknown numbers; the first and the last unknown are always among them.
All inputs are finite; a program needn't handle non-finite values.
Results may differ from a plain program's by a relative error of at most 0.0045.
The roundings to bfloat16 on the way count: a program that leaves them out, or rounds other values in their place, can miss the bound.
Values may be sent and summed in bfloat16 or wider, within the bound.
No kernel may reach another device: no remote copies, remote signals or barrier semaphores. Data moves between devices by JAX's collectives and lax.ppermute only.
A program may use at most 64 MiB of HBM per device.

v0:
```python
import jax
import jax.numpy as jnp
from jax import lax
from jax.sharding import PartitionSpec as P

ITERS = 2


NOISE = 0.5


def from_root(block, axis, holder):
    block = jnp.where(lax.axis_index(axis) == holder, block, jnp.zeros_like(block))
    return lax.psum(block, axis)


def contract(former, latter, shared_axis):
    return lax.dot_general(
        former,
        latter,
        (((shared_axis,), (shared_axis,)), ((), ())),
        preferred_element_type=jnp.float32,
    )


def full_dot(former, latter):
    return jnp.dot(
        former, latter, precision=lax.Precision.HIGHEST, preferred_element_type=jnp.float32
    )


def kernel_block(former, latter):
    former_norm = jnp.sum(jnp.square(former.astype(jnp.float32)), axis=1)
    latter_norm = jnp.sum(jnp.square(latter.astype(jnp.float32)), axis=1)
    between = contract(former, latter, 1)
    return jnp.exp(-0.5 * (former_norm[:, None] + latter_norm[None, :] - 2.0 * between))


def pivot_table(all_points, pivots):
    features = all_points.shape[1]
    owner_ids = pivots // (features + 1)
    component = pivots % (features + 1)
    pivot_pts = jnp.take(all_points, owner_ids, axis=0)
    valued = (component == 0).astype(jnp.float32)
    unit_dirs = (component[:, None] - 1 == jnp.arange(features, dtype=jnp.int32)[None, :]).astype(
        jnp.bfloat16
    )
    chosen = jnp.sum(pivot_pts.astype(jnp.float32) * unit_dirs.astype(jnp.float32), axis=1)
    return (pivot_pts, valued, unit_dirs, chosen)


def factor_rows(own_points, pivot_data):
    pivot_pts, valued, unit_dirs, chosen = pivot_data
    kernel = kernel_block(own_points, pivot_pts)
    along_dirs = contract(own_points, unit_dirs, 1) - chosen[None, :]
    leading = kernel * (valued[None, :] + along_dirs)
    offsets = (
        own_points.astype(jnp.float32)[:, :, None]
        - jnp.transpose(pivot_pts.astype(jnp.float32))[None, :, :]
    )
    slopes = (
        kernel[:, None, :] * jnp.transpose(unit_dirs.astype(jnp.float32))[None, :, :]
        - offsets * leading[:, None, :]
    )
    return (leading.astype(jnp.bfloat16), slopes.astype(jnp.bfloat16))


def pivot_block(pivot_data):
    pivot_pts, valued, unit_dirs, chosen = pivot_data
    kernel = kernel_block(pivot_pts, pivot_pts)
    select = contract(pivot_pts, unit_dirs, 1)
    after_terms = select - chosen[None, :]
    before = chosen[:, None] - jnp.transpose(select)
    unit_dots = contract(unit_dirs, unit_dirs, 1)
    mixed_terms = (
        valued[:, None] * valued[None, :] + valued[:, None] * after_terms - valued[None, :] * before
    )
    return kernel * (mixed_terms + unit_dots - before * after_terms)


def solve_inner(chol_factor, target):
    middle = lax.linalg.triangular_solve(chol_factor, target, left_side=True, lower=True)
    return lax.linalg.triangular_solve(
        chol_factor, middle, left_side=True, lower=True, transpose_a=True
    )


def per_sample(array_in, samples):
    return jnp.sum(array_in.reshape(array_in.shape[0], -1, samples), axis=(0, 1))


def project(leading, slopes, values_here, derivs_here):
    point_count, features, rank_count = slopes.shape
    samples = values_here.shape[1]
    flat_slopes = slopes.reshape(point_count * features, rank_count)
    half_derivs = derivs_here.astype(jnp.bfloat16).reshape(point_count * features, samples)
    projection = contract(leading, values_here.astype(jnp.bfloat16), 0) + contract(
        flat_slopes, half_derivs, 0
    )
    squares = jnp.sum(values_here * values_here, axis=0) + per_sample(
        derivs_here * derivs_here, samples
    )
    return (projection, squares)


def descend(chol_factor, projection, leading, slopes, values_here, derivs_here):
    point_count, features, rank_count = slopes.shape
    coefficients = solve_inner(chol_factor, projection)
    flat_slopes = slopes.reshape(point_count * features, rank_count)
    new_values = (values_here - full_dot(leading, coefficients)) / NOISE
    new_derivs = (
        derivs_here - full_dot(flat_slopes, coefficients).reshape(point_count, -1)
    ) / NOISE
    return (coefficients, new_values, new_derivs)


def tile_image(row_points, col_points, col_search, samples):
    row_total, features = row_points.shape
    col_total = col_points.shape[0]
    pair_count = samples // 2
    kmat = kernel_block(row_points, col_points)
    head_all = col_search[:, :samples]
    slope_all = col_search[:, samples:]
    base_terms = full_dot(kmat, slope_all)
    slope_groups = slope_all.reshape(col_total, features, pair_count, 2)
    owned_all = jnp.sum(col_points.astype(jnp.float32)[:, :, None, None] * slope_groups, axis=1)
    head_groups = jnp.transpose(head_all.reshape(col_total, pair_count, 2), (1, 0, 2))
    slope_pairs = jnp.transpose(slope_groups, (2, 0, 1, 3))
    owned_groups = jnp.transpose(owned_all, (1, 0, 2))

    def one_pair(pair_items):
        head_vals, slopes_here, owned_dots = pair_items
        cross_terms = jnp.einsum(
            "td,cds->tsc",
            row_points,
            slopes_here,
            precision=lax.Precision.HIGHEST,
            preferred_element_type=jnp.float32,
        )
        weight = kmat[:, None, :] * (
            jnp.transpose(head_vals)[None, :, :]
            + cross_terms
            - jnp.transpose(owned_dots)[None, :, :]
        )
        summed = jnp.sum(weight, axis=2)
        moved_sum = jnp.einsum(
            "tsc,cd->tsd",
            weight,
            col_points,
            precision=lax.Precision.HIGHEST,
            preferred_element_type=jnp.float32,
        )
        return (summed, moved_sum)

    summed, moved_sum = lax.map(one_pair, (head_groups, slope_pairs, owned_groups))
    image_values = jnp.transpose(summed, (1, 0, 2)).reshape(row_total, samples)
    extra_terms = jnp.transpose(moved_sum, (1, 3, 0, 2)).reshape(row_total, features * samples)
    image_derivs = (
        base_terms
        - (row_points.astype(jnp.float32)[:, :, None] * image_values[:, None, :]).reshape(
            row_total, -1
        )
        + extra_terms
    )
    return jnp.concatenate([image_values, image_derivs], axis=1)


def local(points, pivots, right_values, right_derivs):
    row_count = lax.axis_size("row")
    col_count = lax.axis_size("col")
    col_index = lax.axis_index("col")
    row_span = row_count // col_count
    local_points, features = points.shape
    samples = right_values.shape[1]
    share_rows = local_points // col_count
    share_start = col_index * share_rows
    all_points = lax.all_gather(points, "row", axis=0, tiled=True)
    col_points = lax.dynamic_slice_in_dim(
        all_points, col_index * (local_points * row_span), local_points * row_span, 0
    )
    own_points = lax.dynamic_slice_in_dim(points, share_start, share_rows, 0)
    pivot_data = pivot_table(all_points, pivots)
    leading, slopes = factor_rows(own_points, pivot_data)
    flat_slopes = slopes.reshape(share_rows * features, -1)
    gram_local = contract(leading, leading, 0) + contract(flat_slopes, flat_slopes, 0)
    first_values = lax.dynamic_slice_in_dim(right_values, share_start, share_rows, 0)
    first_derivs = lax.dynamic_slice_in_dim(right_derivs, share_start, share_rows, 0)
    proj_local, squares_local = project(leading, slopes, first_values, first_derivs)
    gram, first_proj, first_squares = lax.psum(
        (gram_local, proj_local, squares_local), ("row", "col")
    )
    chol_factor = jnp.linalg.cholesky(NOISE * pivot_block(pivot_data) + gram)

    def precondition(projection, values_here, derivs_here):
        coefficients, new_values, new_derivs = descend(
            chol_factor, projection, leading, slopes, values_here, derivs_here
        )
        local_dot = jnp.sum(values_here * new_values, axis=0) + per_sample(
            derivs_here * new_derivs, samples
        )
        gamma_new = lax.psum(local_dot, ("row", "col"))
        return (gamma_new, new_values, new_derivs)

    def widen(values_here, derivs_here):
        return (
            lax.all_gather(values_here, "col", axis=0, tiled=True),
            lax.all_gather(derivs_here, "col", axis=0, tiled=True),
        )

    gamma_now, new_values, new_derivs = precondition(first_proj, first_values, first_derivs)
    search_values, search_derivs = widen(new_values, new_derivs)
    remain_values, remain_derivs = (right_values, right_derivs)
    estimate_values = jnp.zeros_like(right_values)
    estimate_derivs = jnp.zeros_like(right_derivs)
    for iteration in range(ITERS):
        search_all = jnp.concatenate([search_values, search_derivs], axis=1)
        pieces = from_root(search_all, "row", col_index * row_span + 0)
        partial_image = tile_image(points, col_points, pieces, samples)
        image_all = lax.psum(partial_image, "col") + NOISE * search_all
        image_values = image_all[:, :samples]
        image_derivs = image_all[:, samples:]
        local_curve = jnp.sum(search_values * image_values, axis=0) + per_sample(
            search_derivs * image_derivs, samples
        )
        curvature = lax.psum(local_curve, "row")
        step_size = gamma_now / curvature
        tiled_step = jnp.tile(step_size, features)
        estimate_values = estimate_values + step_size * search_values
        estimate_derivs = estimate_derivs + tiled_step * search_derivs
        remain_values = remain_values - step_size * image_values
        remain_derivs = remain_derivs - tiled_step * image_derivs
        if iteration + 1 < ITERS:
            share_values = lax.dynamic_slice_in_dim(remain_values, share_start, share_rows, 0)
            share_derivs = lax.dynamic_slice_in_dim(remain_derivs, share_start, share_rows, 0)
            proj_here, squares_here = project(leading, slopes, share_values, share_derivs)
            refresh_projection, squares = lax.psum((proj_here, squares_here), ("row", "col"))
            gamma_next, new_values, new_derivs = precondition(
                refresh_projection, share_values, share_derivs
            )
            precond_values, precond_derivs = widen(new_values, new_derivs)
            beta_ratio = gamma_next / gamma_now
            search_values = precond_values + beta_ratio * search_values
            search_derivs = precond_derivs + jnp.tile(beta_ratio, features) * search_derivs
            gamma_now = gamma_next
    estimate_values = lax.dynamic_slice_in_dim(estimate_values, share_start, share_rows, 0)
    estimate_derivs = lax.dynamic_slice_in_dim(estimate_derivs, share_start, share_rows, 0)
    remain_values = lax.dynamic_slice_in_dim(remain_values, share_start, share_rows, 0)
    remain_derivs = lax.dynamic_slice_in_dim(remain_derivs, share_start, share_rows, 0)
    return (estimate_values, estimate_derivs, remain_values, remain_derivs)


def solution(mesh):
    in_specs = (P("row", None), P(), P("row", None), P("row", None))
    out_specs = (
        P(("row", "col"), None),
        P(("row", "col"), None),
        P(("row", "col"), None),
        P(("row", "col"), None),
    )
    return jax.shard_map(local, mesh=mesh, in_specs=in_specs, out_specs=out_specs, check_vma=False)
```

profile of v0, /device:TPU:1, one launch (start us, length us, event | category | flops | bytes accessed | tf_op | source)
XLA Modules:
  0.0 1579.1 jit_solution(16942778609122132722)
XLA Ops:
  9.5 43.5 %all_gather.15 = bf16[4096,64]{1,0:T(8,128)(2,1)S(1)} all-gather(bf16[256,64]{1,0:T(8,128)(2,1)S(1)} %copy.64), channel_id=1, replica_groups=mesh['row'=16,'col'=16] {'row'}, dimensions={0}, use_global_device_ids=true | all-gather | bytes 557056 | tf_op jit(solution)/shard_map/all_gather | solution.py:177
  66.2 82.0 %psum.78 = f32[512,16]{0,1:T(8,128)} all-reduce(f32[512,16]{0,1:T(8,128)} %convolution_add_fusion.3), channel_id=1, replica_groups=mesh['row'=16,'col'=16] {'row','col'}, use_global_device_ids=true, to_apply=%region_12.13 | all-reduce | flops 8192 | bytes 65536 | tf_op jit(solution)/shard_map/psum | solution.py:189
  151.0 167.9 %all-reduce.7.cloned.1.call-done = f32[512,512]{1,0:T(8,128)} async-done(((f32[512,512]{1,0:T(8,128)}), f32[512,512]{1,0:T(8,128)}) %all-reduce.7.cloned.1.call-update) | async-done | bytes 1048592 | tf_op jit(solution)/shard_map/psum | solution.py:189
  322.6 11.7 cholesky.104
  346.2 11.7 cholesky.217
  358.4 9.9 custom-call.34
  369.9 11.7 cholesky.238
  392.8 12.1 cholesky.255
  409.8 10.4 while.34
  420.2 40.2 %custom-call.39 = f32[4,128,128]{1,2,0:T(8,128)S(1)} custom-call(f32[4,128,128]{2,1,0:T(8,128)} %get-tuple-element.135), custom_call_target="InvertDiagBlocksLowerTriangular" | custom-call | tf_op jit(solution)/shard_map/triangular_solve/custom-call.8 | solution.py:83
  470.4 32.6 %all_gather.16 = f32[256,16]{1,0:T(8,128)S(1)} all-gather(f32[16,16]{1,0:T(8,128)S(1)} %get-tuple-element.282), channel_id=1, replica_groups=mesh['row'=16,'col'=16] {'col'}, dimensions={0}, use_global_device_ids=true | all-gather | bytes 17408 | tf_op jit(solution)/shard_map/all_gather | solution.py:206
  502.9 23.0 %all-gather.3.cloned.1.call-done = f32[256,1024]{1,0:T(8,128)} async-done(((f32[16,1024]{1,0:T(8,128)}), f32[256,1024]{1,0:T(8,128)}) %all-gather.3.cloned.1.call-update) | async-done | bytes 1048592 | tf_op jit(solution)/shard_map/all_gather | solution.py:207
  530.1 147.6 %all-reduce.9.cloned.1.call-done = f32[256,1040]{1,0:T(8,128)} async-done(((f32[256,1040]{1,0:T(8,128)}), f32[256,1040]{1,0:T(8,128)}) %all-reduce.9.cloned.1.call-update) | async-done | bytes 1064976 | tf_op jit(solution)/shard_map/psum | solution.py:14
  684.3 12.2 while.32
  709.7 86.9 %psum.79 = f32[16]{0:T(128)} all-reduce(f32[16]{0:T(128)S(1)} %add.241), channel_id=1, replica_groups=mesh['row'=16,'col'=16] {'row','col'}, use_global_device_ids=true, to_apply=%region_16.19 | all-reduce | flops 16 | bytes 128 | tf_op jit(solution)/shard_map/psum | solution.py:201
  796.6 102.6 %all-reduce.11.cloned.1.call-done = f32[256,1040]{1,0:T(8,128)} async-done(((f32[256,1040]{1,0:T(8,128)}), f32[256,1040]{1,0:T(8,128)}) %all-reduce.11.cloned.1.call-update) | async-done | bytes 1064976 | tf_op jit(solution)/shard_map/psum | solution.py:219
  906.2 34.9 %psum.82 = f32[16]{0:T(128)} all-reduce(f32[16]{0:T(128)} %add.248), channel_id=1, replica_groups=mesh['row'=16,'col'=16] {'row'}, use_global_device_ids=true, to_apply=%region_28.31 | all-reduce | flops 16 | bytes 128 | tf_op jit(solution)/shard_map/psum | solution.py:225
  951.4 80.1 %psum.83 = f32[512,16]{0,1:T(8,128)S(1)} all-reduce(f32[512,16]{0,1:T(8,128)S(1)} %convolution_add_fusion.2), channel_id=1, replica_groups=mesh['row'=16,'col'=16] {'row','col'}, use_global_device_ids=true, to_apply=%region_29.32 | all-reduce | flops 8192 | bytes 65536 | tf_op jit(solution)/shard_map/psum | solution.py:236
  1043.3 77.9 %psum.84 = f32[16]{0:T(128)S(1)} all-reduce(f32[16]{0:T(128)S(1)} %add.250), channel_id=1, replica_groups=mesh['row'=16,'col'=16] {'row','col'}, use_global_device_ids=true, to_apply=%region_33.36 | all-reduce | flops 16 | bytes 128 | tf_op jit(solution)/shard_map/psum | solution.py:201
  1121.7 28.6 %all_gather.18 = f32[256,16]{1,0:T(8,128)S(1)} all-gather(f32[16,16]{1,0:T(8,128)S(1)} %get-tuple-element.284), channel_id=1, replica_groups=mesh['row'=16,'col'=16] {'col'}, dimensions={0}, use_global_device_ids=true | all-gather | bytes 17408 | tf_op jit(solution)/shard_map/all_gather | solution.py:206
  1153.4 147.1 %all-reduce.13.cloned.1.call-done = f32[256,1040]{1,0:T(8,128)} async-done(((f32[256,1040]{1,0:T(8,128)}), f32[256,1040]{1,0:T(8,128)}) %all-reduce.13.cloned.1.call-update) | async-done | bytes 1064976 | tf_op jit(solution)/shard_map/psum | solution.py:14
  1310.8 17.7 %while.33 = (s32[]{:T(128)}, f32[8,256,2]{1,2,0:T(2,128)S(1)}, f32[8,256,2,64]{1,3,2,0:T(8,128)}, f32[256,256]{0,1:T(8,128)S(1)}, f32[8,256,2]{1,2,0:T(2,128)}, ...) while((s32[]{:T(128)}, f32[8,256,2]{1,2,0:T(2,128)S(1)}, ...), condition=%wide.region_38.41_spmd, body=%wide.region_36.40_spmd.sunk | while | flops 201850368 | bytes 1919601 | solution.py:155
  1342.6 190.0 %all-reduce.15.cloned.1.call-done = f32[256,1040]{1,0:T(8,128)} async-done(((f32[256,1040]{1,0:T(8,128)}), f32[256,1040]{1,0:T(8,128)}) %all-reduce.15.cloned.1.call-update) | async-done | bytes 1064976 | tf_op jit(solution)/shard_map/psum | solution.py:219
  1534.8 34.3 %psum.87 = f32[16]{0:T(128)S(1)} all-reduce(f32[16]{0:T(128)S(1)} %add.255), channel_id=1, replica_groups=mesh['row'=16,'col'=16] {'row'}, use_global_device_ids=true, to_apply=%region_43.46 | all-reduce | flops 16 | bytes 128 | tf_op jit(solution)/shard_map/psum | solution.py:225
  (373 shorter events, 184.6 us)
Async XLA Ops:
  7.2 311.7 %all-reduce.7.cloned.1.call-start = ((), (), s32[]{:S(2)}) async-start(), calls=%async_computation | async-start | bytes 2097152 | tf_op jit(solution)/shard_map/psum | solution.py:189
  7.9 47.7 %copy-start.36 = (f32[512]{0:T(512)}, f32[512]{0:T(512)S(1)}, u32[]{:S(2)}) copy-start(f32[512]{0:T(512)S(1)} %get-tuple-element.274) | copy-start | bytes 6148
  7.9 50.7 %copy-start.39 = (pred[512]{0:T(512)(128)(4,1)}, pred[512]{0:T(512)(128)(4,1)S(1)}, u32[]{:S(2)}) copy-start(pred[512]{0:T(512)(128)(4,1)S(1)} %get-tuple-element.244) | copy-start | bytes 1540
  8.6 50.0 %copy-start.31 = (s32[512]{0:T(512)}, s32[512]{0:T(512)S(1)}, u32[]{:S(2)}) copy-start(s32[512]{0:T(512)S(1)} %broadcast_add_fusion) | copy-start | bytes 6148
  58.6 467.3 %all-gather.3.cloned.1.call-start = ((), (), s32[]{:S(2)}) async-start(), calls=%async_computation.1 | async-start | bytes 1114112 | tf_op jit(solution)/shard_map/all_gather | solution.py:207
  62.1 407.5 %copy-start.27 = (f32[256,16]{1,0:T(8,128)}, f32[256,16]{1,0:T(8,128)S(1)}, u32[]{:S(2)}) copy-start(f32[256,16]{1,0:T(8,128)S(1)} %copy.63) | copy-start | bytes 49156
  148.6 170.3 %copy-start.34 = (f32[512]{0:T(512)S(1)}, f32[512]{0:T(512)}, u32[]{:S(2)}) copy-start(f32[512]{0:T(512)} %copy-done.33) | copy-start | bytes 6148
  148.6 170.3 %copy-start.40 = (pred[512]{0:T(512)(128)(4,1)S(1)}, pred[512]{0:T(512)(128)(4,1)}, u32[]{:S(2)}) copy-start(pred[512]{0:T(512)(128)(4,1)} %copy-done.39) | copy-start | bytes 1540
  420.2 46.9 %copy-start.2 = (f32[512,512]{1,0:T(8,128)}, f32[512,512]{1,0:T(8,128)S(1)}, u32[]{:S(2)}) copy-start(f32[512,512]{1,0:T(8,128)S(1)} %get-tuple-element.527) | copy-start | bytes 3145732
  469.5 208.1 %all-reduce.9.cloned.1.call-start = ((), (), s32[]{:S(2)}) async-start(), calls=%async_computation.2 | async-start | bytes 2359296 | tf_op jit(solution)/shard_map/psum | solution.py:14
  528.6 370.6 %all-reduce.11.cloned.1.call-start = ((), (), s32[]{:S(2)}) async-start(), calls=%async_computation.3 | async-start | bytes 2359296 | tf_op jit(solution)/shard_map/psum | solution.py:219
  529.7 152.9 %copy-start.25 = (f32[256,64]{0,1:T(8,128)}, f32[256,64]{0,1:T(8,128)S(1)}, u32[]{:S(2)}) copy-start(f32[256,64]{0,1:T(8,128)S(1)} %copy.73) | copy-start | bytes 196612
  529.8 171.1 %copy-start.23 = (f32[256,64]{0,1:T(8,128)}, f32[256,64]{0,1:T(8,128)S(1)}, u32[]{:S(2)}) copy-start(f32[256,64]{0,1:T(8,128)S(1)} %convert_element_type.102) | copy-start | bytes 196612
  708.9 190.3 %copy-start = (f32[256,1024]{1,0:T(8,128)S(1)}, f32[256,1024]{1,0:T(8,128)}, u32[]{:S(2)}) copy-start(f32[256,1024]{1,0:T(8,128)} %all-gather.3.cloned.1.call-done) | copy-start | bytes 3145732
  708.9 441.5 %all-gather.5.cloned.1.call-start = ((), (), s32[]{:S(2)}) async-start(), calls=%async_computation.4 | async-start | bytes 1114112 | tf_op jit(solution)/shard_map/all_gather | solution.py:207
  948.0 84.5 %copy-start.3 = (f32[512,512]{1,0:T(8,128)S(1)}, f32[512,512]{1,0:T(8,128)}, u32[]{:S(2)}) copy-start(f32[512,512]{1,0:T(8,128)} %copy-done.2) | copy-start | bytes 3145732
  1039.5 81.8 %copy-start.47 = (f32[16]{0:T(128)S(1)}, f32[16]{0:T(128)}, u32[]{:S(2)}) copy-start(f32[16]{0:T(128)} %psum.79) | copy-start | bytes 196
  1039.5 110.9 %copy-start.16 = (f32[256,16]{1,0:T(8,128)S(1)}, f32[256,16]{1,0:T(8,128)}, u32[]{:S(2)}) copy-start(f32[256,16]{1,0:T(8,128)} %copy-done.14) | copy-start | bytes 49156
  1042.3 258.2 %all-reduce.13.cloned.1.call-start = ((), (), s32[]{:S(2)}) async-start(), calls=%async_computation.5 | async-start | bytes 2359296 | tf_op jit(solution)/shard_map/psum | solution.py:14
  1153.4 379.2 %all-reduce.15.cloned.1.call-start = ((), (), s32[]{:S(2)}) async-start(), calls=%async_computation.6 | async-start | bytes 2359296 | tf_op jit(solution)/shard_map/psum | solution.py:219
  1342.6 190.0 %copy-start.20 = (f32[256,16]{1,0:T(8,128)S(1)}, f32[256,16]{1,0:T(8,128)}, u32[]{:S(2)}) copy-start(f32[256,16]{1,0:T(8,128)} %copy-done.19) | copy-start | bytes 49156
  1534.2 34.9 %copy-start.44 = (f32[16]{0:T(128)S(1)}, f32[16]{0:T(128)}, u32[]{:S(2)}) copy-start(f32[16]{0:T(128)} %copy-done.43) | copy-start | bytes 196
  1534.2 34.9 %copy-start.42 = (f32[16]{0:T(128)S(1)}, f32[16]{0:T(128)}, u32[]{:S(2)}) copy-start(f32[16]{0:T(128)} %copy-done.41) | copy-start | bytes 196
  1534.2 36.3 %copy-start.32 = (f32[1024]{0:T(1024)S(1)}, f32[1024]{0:T(1024)}, u32[]{:S(2)}) copy-start(f32[1024]{0:T(1024)} %mul.352) | copy-start | bytes 12292
  (32 other events, 150.2 us)
Sparse Core Ops, SparseCore 0:
  58.7 260.1 all-reduce.6
  469.7 56.2 all-gather.2
  528.8 148.8 all-reduce.8
  709.0 190.1 all-reduce.10
  1042.4 51.6 all-gather.4
  1153.5 146.9 all-reduce.12
  1342.7 189.8 all-reduce.14
where the time goes:
time: 1590 us; the launch traced here: 1580 us
  waiting for transfers between devices  778 us (49%)
  blocking collectives  501 us (32%)
  other arithmetic  159 us (10%)
  local copies, waits for them, and re-layouts  61.9 us (4%)
  matrix products  60.6 us (4%)
  between operations  17.9 us (1%)
    psum x2, waiting for transfers between devices, from_root(): return lax.psum(block, axis)  295 us
    psum x2, waiting for transfers between devices, local(): image_all = lax.psum(partial_image, 'col') + NOISE * search_all  293 us
    psum x1, waiting for transfers between devices, local(): lax.psum((gram_local, proj_local, squares_local), ('row', 'col'))  168 us
    psum x2, blocking collectives, precondition(): gamma_new = lax.psum(local_dot, ('row', 'col'))  165 us
    psum x1, blocking collectives, local(): lax.psum((gram_local, proj_local, squares_local), ('row', 'col'))  82 us
    another operation x14, other arithmetic, local(): chol_factor = jnp.linalg.cholesky(NOISE * pivot_block(pivot_data) + gram)  80.7 us
    psum x1, blocking collectives, local(): lax.psum((proj_here, squares_here), ('row', 'col'))  80.1 us
    psum x2, blocking collectives, local(): curvature = lax.psum(local_curve, 'row')  69.2 us
  transfers between devices with their start and end apart: 7, of which 6 were waited for; matrix products, arithmetic and copies ran while one was open for 1% of the time, Pallas kernels for 0%

commit v1 on v0

v1 whole, which is shorter than its diff:
```python
import jax
import jax.numpy as jnp
from jax import lax
from jax.sharding import PartitionSpec as P

ITERS = 2
NOISE = 0.5
HIGHEST = lax.Precision.HIGHEST


def spread(block, axis):
    copies = jnp.broadcast_to(block[None], (lax.axis_size(axis),) + block.shape)
    return lax.all_to_all(copies, axis, 0, 0, tiled=True)


def wide_dot(former, latter, dims):
    return lax.dot_general(
        former.astype(jnp.float32),
        latter.astype(jnp.float32),
        ((dims[0:1], dims[1:2]), ((), ())),
        precision=HIGHEST,
        preferred_element_type=jnp.float32,
    )


def half_dot(former, latter, dims):
    return lax.dot_general(
        former,
        latter,
        ((dims[0:1], dims[1:2]), ((), ())),
        preferred_element_type=jnp.float32,
    )


def pivot_table(all_points, pivots):
    count, features = all_points.shape
    owner_ids = pivots // (features + 1)
    component = pivots % (features + 1)
    picks = (owner_ids[:, None] == jnp.arange(count, dtype=jnp.int32)[None, :]).astype(jnp.bfloat16)
    pivot_pts = half_dot(picks, all_points, (1, 0)).astype(jnp.bfloat16)
    valued = (component == 0).astype(jnp.float32)
    unit_dirs = (component[:, None] - 1 == jnp.arange(features, dtype=jnp.int32)[None, :]).astype(
        jnp.bfloat16
    )
    chosen = jnp.sum(pivot_pts.astype(jnp.float32) * unit_dirs.astype(jnp.float32), axis=1)
    return (pivot_pts, valued, unit_dirs, chosen)


def square_norms(points):
    return jnp.sum(jnp.square(points.astype(jnp.float32)), axis=1)


def factor_rows(own_points, pivot_data):
    pivot_pts, valued, unit_dirs, chosen = pivot_data
    norms = square_norms(own_points)
    dots = half_dot(own_points, pivot_pts, (1, 1))
    kern = jnp.exp(-0.5 * (norms[:, None] + square_norms(pivot_pts)[None, :] - 2.0 * dots))
    along = half_dot(own_points, unit_dirs, (1, 1)) - chosen[None, :]
    lead = kern * (valued[None, :] + along)
    offsets = (
        jnp.transpose(own_points.astype(jnp.float32))[:, :, None]
        - jnp.transpose(pivot_pts.astype(jnp.float32))[:, None, :]
    )
    slopes = (
        kern[None] * jnp.transpose(unit_dirs.astype(jnp.float32))[:, None, :] - offsets * lead[None]
    )
    return jnp.concatenate([lead[None], slopes], axis=0).astype(jnp.bfloat16)


def pivot_block(pivot_data):
    pivot_pts, valued, unit_dirs, chosen = pivot_data
    norms = square_norms(pivot_pts)
    dots = half_dot(pivot_pts, pivot_pts, (1, 1))
    kernel = jnp.exp(-0.5 * (norms[:, None] + norms[None, :] - 2.0 * dots))
    select = half_dot(pivot_pts, unit_dirs, (1, 1))
    after_terms = select - chosen[None, :]
    before = chosen[:, None] - jnp.transpose(select)
    unit_dots = half_dot(unit_dirs, unit_dirs, (1, 1))
    mixed_terms = (
        valued[:, None] * valued[None, :] + valued[:, None] * after_terms - valued[None, :] * before
    )
    return kernel * (mixed_terms + unit_dots - before * after_terms)


def thirds(wide):
    high = lax.reduce_precision(wide, 8, 7)
    middle = lax.reduce_precision(wide - high, 8, 7)
    low = wide - high - middle
    return jnp.stack([high, middle, low]).astype(jnp.bfloat16)


def project(flat_factor, field):
    parts = half_dot(thirds(field.reshape(-1)), flat_factor, (1, 0))
    return jnp.stack([parts[0], parts[0] + (parts[1] + parts[2])])


def expand(flat_factor, coef):
    parts = half_dot(thirds(coef), flat_factor, (1, 1))
    return parts[0] + (parts[1] + parts[2])


def operate(row_points, kmat, points, field, row_field):
    values, derivs = field[:, 0], field[:, 1:]
    owned = values - jnp.sum(points.astype(jnp.float32) * derivs, axis=1)
    weight = kmat * (wide_dot(row_points, derivs, (1, 1)) + owned[None, :])
    moved = wide_dot(weight, points, (1, 0))
    summed = jnp.sum(weight, axis=1, keepdims=True)
    base = wide_dot(kmat, derivs, (1, 0))
    return (
        jnp.concatenate([summed, base - row_points.astype(jnp.float32) * summed + moved], axis=1)
        + NOISE * row_field
    )


def local(points, pivots, right_values, right_derivs):
    row, col = lax.axis_index("row"), lax.axis_index("col")
    row_count, col_count = lax.axis_size("row"), lax.axis_size("col")
    row_total, features = points.shape
    samples = right_values.shape[1]
    rank = pivots.shape[0]
    width = features + 1

    def assemble(blocks):
        return jnp.transpose(blocks, (0, 2, 1)).reshape(row_count * row_total, width)

    all_points = spread(points, "row").reshape(-1, features)
    lanes = jnp.arange(samples * features, dtype=jnp.int32)
    picks = (lanes[None, :] == jnp.arange(features, dtype=jnp.int32)[:, None] * samples + col)
    value_picks = (jnp.arange(samples, dtype=jnp.int32) == col)[None, :]
    residual = jnp.concatenate(
        [wide_dot(value_picks, right_values, (1, 1)), wide_dot(picks, right_derivs, (1, 1))],
        axis=0,
    )

    pivot_data = pivot_table(all_points, pivots)
    factor = factor_rows(points, pivot_data).reshape(width * row_total, rank)
    share = rank // col_count
    block = lax.dynamic_slice_in_dim(factor, col * share, share, 1)
    gram_part = half_dot(block, factor, (0, 0))
    sums = spread(jnp.concatenate([gram_part, project(factor, residual)], axis=0), "row")
    sums = jnp.sum(sums, axis=0)
    gram = spread(sums[:share], "col").reshape(rank, rank)
    chol = jnp.linalg.cholesky(NOISE * pivot_block(pivot_data) + gram)

    def solve(target):
        middle = lax.linalg.triangular_solve(chol, target[:, None], left_side=True, lower=True)
        return lax.linalg.triangular_solve(
            chol, middle, left_side=True, lower=True, transpose_a=True
        )[:, 0]

    kmat = jnp.exp(
        -0.5
        * (
            square_norms(points)[:, None]
            + square_norms(all_points)[None, :]
            - 2.0 * half_dot(points, all_points, (1, 1))
        )
    )

    def total(part):
        return jnp.sum(spread(part[None], "row"), axis=(0, 1))

    def descend(projections, squares, field):
        coef = solve(projections[0])
        descent = (field - expand(factor, coef).reshape(width, row_total)) / NOISE
        return ((squares - jnp.sum(projections[1] * coef)) / NOISE, descent)

    def image_of(direction):
        whole = assemble(spread(direction, "row"))
        own = jnp.transpose(direction)
        return jnp.transpose(operate(points, kmat, all_points, whole, own))

    squares = total(jnp.broadcast_to(jnp.sum(residual * residual), (128,)))[0]
    gamma, direction = descend(sums[share:], squares, residual)
    estimate = jnp.zeros_like(residual)
    for iteration in range(ITERS):
        image = image_of(direction)
        curve = total(jnp.broadcast_to(jnp.sum(direction * image), (128,)))[0]
        step = gamma / curve
        estimate = estimate + step * direction
        residual = residual - step * image
        if iteration + 1 < ITERS:
            part = jnp.concatenate(
                [
                    project(factor, residual).reshape(-1),
                    jnp.broadcast_to(jnp.sum(residual * residual), (128,)),
                ]
            )
            sums = total(part)
            gamma_next, descent = descend(sums[: 2 * rank].reshape(2, rank), sums[-1], residual)
            direction = descent + (gamma_next / gamma) * direction
            gamma = gamma_next
    share_rows = row_total // col_count
    fields = jnp.stack([estimate, residual]).reshape(2, width, col_count, share_rows)
    fields = jnp.transpose(fields, (2, 0, 1, 3)).reshape(col_count, -1)
    fields = lax.all_to_all(fields, "col", 0, 0, tiled=True)
    fields = jnp.transpose(fields.reshape(samples, 2, width, share_rows), (1, 3, 2, 0))
    values, derivs = fields[:, :, 0], fields[:, :, 1:].reshape(2, share_rows, features * samples)
    return (values[0], derivs[0], values[1], derivs[1])


def solution(mesh):
    in_specs = (P("row", None), P(), P("row", None), P("row", None))
    out_specs = (P(("row", "col"), None),) * 4
    return jax.shard_map(local, mesh=mesh, in_specs=in_specs, out_specs=out_specs, check_vma=False)
```

time: 1590 us -> 476 us (0.30)
  waiting for transfers between devices: 778 us -> 58.8 us
  blocking collectives: 501 us -> 93.9 us
  starting transfers between devices: 0.29 us -> 52 us
  local copies, waits for them, and re-layouts: 61.9 us -> 36.1 us
    psum x5 -> x0, waiting for transfers between devices: 755 us -> none  [the longest x2 295 us: from_root(): return lax.psum(block, axis)]
    psum x6 -> x0, blocking collectives: 396 us -> none  [the longest x2 165 us: precondition(): gamma_new = lax.psum(local_dot, ('row', 'col'))]
    all_gather x3 -> x0, blocking collectives: 105 us -> none  [the longest x2 61.2 us: widen(): lax.all_gather(values_here, 'col', axis=0, tiled=True)]
    all_to_all x0 -> x4, blocking collectives: none -> 93.9 us  [the longest x3 76.9 us: spread(): return lax.all_to_all(copies, axis, 0, 0, tiled=True)]
    all_to_all x0 -> x6, waiting for transfers between devices: none -> 58.8 us  [spread(): return lax.all_to_all(copies, axis, 0, 0, tiled=True)]
    all_to_all x0 -> x6, starting transfers between devices: none -> 52 us  [spread(): return lax.all_to_all(copies, axis, 0, 0, tiled=True)]
    all_gather x2 -> x0, waiting for transfers between devices: 23 us -> none  [widen(): lax.all_gather(derivs_here, 'col', axis=0, tiled=True)]
    dot_general x50 -> x20, matrix products: 44.1 us -> 64.3 us  [the longest x12 45.6 us: half_dot(): lax.dot_general(former, latter, ((dims[0:1], dims[1:2]), ((), ())), prefe...]
  transfers between devices with their start and end apart: 7 -> 6, of which waited for: 6 -> 5; matrix products, arithmetic and copies ran while one was open for 1% -> 5% of each run, Pallas kernels for 0% -> 0%
where the time goes in v1:
time: 476 us; the launch traced here: 468 us
  other arithmetic  145 us (30%)
  blocking collectives  93.9 us (20%)
  matrix products  75.6 us (16%)
  waiting for transfers between devices  58.8 us (12%)
  starting transfers between devices  52 us (11%)
  local copies, waits for them, and re-layouts  36.1 us (8%)
  between operations  6.61 us (1%)
    another operation x14, other arithmetic, local(): chol = jnp.linalg.cholesky(NOISE * pivot_block(pivot_data) + gram)  78.9 us
    all_to_all x3, blocking collectives, spread(): return lax.all_to_all(copies, axis, 0, 0, tiled=True)  76.9 us
    all_to_all x6, waiting for transfers between devices, spread(): return lax.all_to_all(copies, axis, 0, 0, tiled=True)  58.8 us
    all_to_all x6, starting transfers between devices, spread(): return lax.all_to_all(copies, axis, 0, 0, tiled=True)  52 us
    dot_general x12, matrix products, half_dot(): lax.dot_general(former, latter, ((dims[0:1], dims[1:2]), ((), ())), prefe...  45.6 us
    another operation x4, other arithmetic, solve(): lax.linalg.triangular_solve(chol, middle, left_side=True, lower=True, tra...  40.3 us
    dot_general x8, matrix products, wide_dot(): lax.dot_general(former.astype(jnp.float32), latter.astype(jnp.float32), (...  18.8 us
    all_to_all x1, blocking collectives, local(): fields = lax.all_to_all(fields, 'col', 0, 0, tiled=True)  17 us
  transfers between devices with their start and end apart: 6, of which 5 were waited for; matrix products, arithmetic and copies ran while one was open for 5% of the time, Pallas kernels for 0%

profile of v1, /device:TPU:1, one launch (start us, length us, event | category | flops | bytes accessed | tf_op | source)
XLA Modules:
  0.0 468.0 jit_solution(3701869973653993978)
XLA Ops:
  2.3 9.2 %all-to-all-start = ((bf16[16,256,64]{1,2,0:T(8,128)(2,1)}), bf16[16,256,64]{1,2,0:T(8,128)(2,1)S(1)}, u32[]{:S(2)}, u32[]{:S(2)}) async-start(bf16[16,256,64]{1,2,0:T(8,128)(2,1)} %broadcast_in_dim.26), calls=%async_computation | async-start | bytes 1048576 | tf_op jit(solution)/shard_map/all_to_all | solution.py:13
  16.3 9.0 %all-to-all-done = bf16[16,256,64]{1,2,0:T(8,128)(2,1)S(1)} async-done(((bf16[16,256,64]{1,2,0:T(8,128)(2,1)}), bf16[16,256,64]{1,2,0:T(8,128)(2,1)S(1)}, u32[]{:S(2)}, u32[]{:S(2)}) %all-to-all-start) | async-done | bytes 524320 | tf_op jit(solution)/shard_map/all_to_all | solution.py:13
  35.5 8.2 %pad_maximum_fusion = bf16[65,256,512]{2,1,0:T(8,128)(2,1)S(1)} fusion(bf16[64,256,512]{2,1,0:T(8,128)(2,1)} %subtract_convert_fusion, bf16[1,256,512]{2,1,0:T(8,128)(2,1)S(1)} %convert_bitcast_fusion), kind=kLoop, calls=%fused_computation.3 | loop fusion | flops 8519680 | bytes 34078720 | tf_op jit(solution)/shard_map/concatenate | solution.py:67
  53.3 36.4 %all_to_all.55 = f32[16,34,512]{2,1,0:T(8,128)S(1)} all-to-all(f32[16,34,512]{2,1,0:T(8,128)S(1)} %broadcast_in_dim.28), channel_id=1, replica_groups=mesh['row'=16,'col'=16] {'row'}, dimensions={0} | all-to-all | bytes 2228224 | tf_op jit(solution)/shard_map/all_to_all | solution.py:13
  91.0 11.0 %all-to-all-start.2 = ((f32[16,32,512]{2,1,0:T(8,128)}), f32[16,32,512]{2,1,0:T(8,128)S(1)}, u32[]{:S(2)}, u32[]{:S(2)}) async-start(f32[16,32,512]{2,1,0:T(8,128)} %broadcast_in_dim.29), calls=%async_computation.2 | async-start | bytes 2097152 | tf_op jit(solution)/shard_map/all_to_all | solution.py:13
  106.4 17.5 %all-to-all-done.2 = f32[16,32,512]{2,1,0:T(8,128)S(1)} async-done(((f32[16,32,512]{2,1,0:T(8,128)}), f32[16,32,512]{2,1,0:T(8,128)S(1)}, u32[]{:S(2)}, u32[]{:S(2)}) %all-to-all-start.2) | async-done | bytes 1048608 | tf_op jit(solution)/shard_map/all_to_all | solution.py:13
  127.2 11.7 %cholesky.104 = f32[128,128]{1,0:T(8,128)S(1)} custom-call(f32[128,128]{1,0:T(8,128)S(1)} %cholesky.266), custom_call_target="Cholesky" | custom-call | tf_op jit(solution)/shard_map/jit(cholesky)/cholesky | solution.py:143
  139.1 9.8 %custom-call.33 = f32[1,128,128]{1,2,0:T(8,128)S(1)} custom-call(f32[1,128,128]{2,1,0:T(8,128)S(1)} %get-tuple-element.106), custom_call_target="InvertDiagBlocksLowerTriangular" | custom-call | tf_op jit(solution)/shard_map/jit(cholesky)/cholesky | solution.py:143
  151.4 12.1 %cholesky.217 = f32[128,128]{1,0:T(8,128)S(1)} custom-call(f32[128,128]{1,0:T(8,128)S(1)} %cholesky.270), custom_call_target="Cholesky" | custom-call | tf_op jit(solution)/shard_map/jit(cholesky)/cholesky | solution.py:143
  163.5 9.8 %custom-call.34 = f32[1,128,128]{1,2,0:T(8,128)S(1)} custom-call(f32[1,128,128]{2,1,0:T(8,128)S(1)} %get-tuple-element.103), custom_call_target="InvertDiagBlocksLowerTriangular" | custom-call | tf_op jit(solution)/shard_map/jit(cholesky)/cholesky | solution.py:143
  174.9 11.7 %cholesky.238 = f32[128,128]{1,0:T(8,128)S(1)} custom-call(f32[128,128]{1,0:T(8,128)S(1)} %cholesky.275), custom_call_target="Cholesky" | custom-call | tf_op jit(solution)/shard_map/jit(cholesky)/cholesky | solution.py:143
  187.3 9.8 %custom-call.35 = f32[1,128,128]{1,2,0:T(8,128)S(1)} custom-call(f32[1,128,128]{2,1,0:T(8,128)S(1)} %get-tuple-element.100), custom_call_target="InvertDiagBlocksLowerTriangular" | custom-call | tf_op jit(solution)/shard_map/jit(cholesky)/cholesky | solution.py:143
  198.6 11.9 %cholesky.255 = f32[128,128]{1,0:T(8,128)S(1)} custom-call(f32[128,128]{1,0:T(8,128)S(1)} %convolution_subtract_fusion.5), custom_call_target="Cholesky" | custom-call | tf_op jit(solution)/shard_map/jit(cholesky)/cholesky | solution.py:143
  214.4 10.4 %while.8 = (s32[]{:T(128)}, f32[512,512]{1,0:T(8,128)S(1)}, s32[4,2]{0,1:T(2,128)S(1)}, f32[4,128,128]{2,1,0:T(8,128)}, s32[]{:T(128)}) while((s32[]{:T(128)}, f32[512,512]{1,0:T(8,128)S(1)}, s32[4,2]{0,1:T(2,128)S(1)}, f32[4,128,128]{2,1,0:T(8,128)}, s32[]{:T(128)}) %tuple.72), condition=%wide.while_cond.1, body=%wide.while_body.1.sunk | while | flops 2 | bytes 132705 | solution.py:147
  224.8 40.1 %custom-call.39 = f32[4,128,128]{1,2,0:T(8,128)S(1)} custom-call(f32[4,128,128]{2,1,0:T(8,128)} %get-tuple-element.35), custom_call_target="InvertDiagBlocksLowerTriangular" | custom-call | tf_op jit(solution)/shard_map/triangular_solve/custom-call.8 | solution.py:147
  267.9 10.3 %fusion.103 = f32[3,16640]{1,0:T(4,128)S(1)} fusion(bf16[16640,512]{1,0:T(8,128)(2,1)} %bitcast.397, bf16[1,512]{1,0:T(2,128)(2,1)S(1)} %get-tuple-element.114, bf16[1,512]{1,0:T(2,128)(2,1)S(1)} %get-tuple-element.113, bf16[1,512]{1,0:T(2,128)(2,1)S(1)} %get-tuple-element.78), kind=kOutput, calls=%fused_computation.210 | convolution fusion | flops 51127296 | bytes 17242112 | tf_op jit(solution)/shard_map/dot_general | solution.py:27
  280.9 11.8 %all-to-all-start.4 = ((f32[16,65,256]{2,1,0:T(8,128)}), f32[16,65,256]{2,1,0:T(8,128)S(1)}, u32[]{:S(2)}, u32[]{:S(2)}) async-start(f32[16,65,256]{2,1,0:T(8,128)} %broadcast_in_dim.31), calls=%async_computation.4 | async-start | bytes 2359296 | tf_op jit(solution)/shard_map/all_to_all | solution.py:13
  296.8 20.2 %all-to-all-done.4 = f32[16,65,256]{2,1,0:T(8,128)S(1)} async-done(((f32[16,65,256]{2,1,0:T(8,128)}), f32[16,65,256]{2,1,0:T(8,128)S(1)}, u32[]{:S(2)}, u32[]{:S(2)}) %all-to-all-start.4) | async-done | bytes 1064992 | tf_op jit(solution)/shard_map/all_to_all | solution.py:13
  318.2 8.6 %all-to-all-start.3 = ((f32[16,1,128]{2,1,0:T(1,128)}), f32[16,1,128]{2,1,0:T(1,128)S(1)}, u32[]{:S(2)}, u32[]{:S(2)}) async-start(f32[16,1,128]{2,1,0:T(1,128)} %broadcast_in_dim.30), calls=%async_computation.3 | async-start | bytes 16384 | tf_op jit(solution)/shard_map/all_to_all | solution.py:13
  354.3 8.1 %fusion.61 = f32[3,512]{1,0:T(4,128)S(1)} fusion(bf16[16640,512]{1,0:T(8,128)(2,1)} %bitcast.398, bf16[1,16640]{1,0:T(2,128)(2,1)S(1)} %get-tuple-element.91, bf16[1,16640]{1,0:T(2,128)(2,1)S(1)} %get-tuple-element.92, bf16[1,16640]{1,0:T(2,128)(2,1)S(1)} %get-tuple-element.90), kind=kOutput, calls=%fused_computation.126 | convolution fusion | flops 51417600 | bytes 17145344 | tf_op jit(solution)/shard_map/dot_general | solution.py:27
  363.2 10.1 %all_to_all.56 = f32[16,1,1152]{2,1,0:T(1,128)S(1)} all-to-all(f32[16,1,1152]{2,1,0:T(1,128)S(1)} %broadcast_in_dim.34), channel_id=1, replica_groups=mesh['row'=16,'col'=16] {'row'}, dimensions={0} | all-to-all | bytes 147456 | tf_op jit(solution)/shard_map/all_to_all | solution.py:13
  378.9 10.3 %fusion.109 = f32[3,16640]{1,0:T(4,128)S(1)} fusion(bf16[16640,512]{1,0:T(8,128)(2,1)} %bitcast.399, bf16[1,512]{1,0:T(2,128)(2,1)S(1)} %get-tuple-element.112, bf16[1,512]{1,0:T(2,128)(2,1)S(1)} %get-tuple-element.111, bf16[1,512]{1,0:T(2,128)(2,1)S(1)} %get-tuple-element.72), kind=kOutput, calls=%fused_computation.217 | convolution fusion | flops 51127296 | bytes 17242112 | tf_op jit(solution)/shard_map/dot_general | solution.py:27
  389.6 30.4 %all_to_all.57 = f32[16,65,256]{2,1,0:T(8,128)S(1)} all-to-all(f32[16,65,256]{2,1,0:T(8,128)S(1)} %broadcast_in_dim.35), channel_id=1, replica_groups=mesh['row'=16,'col'=16] {'row'}, dimensions={0} | all-to-all | bytes 2129920 | tf_op jit(solution)/shard_map/all_to_all | solution.py:13
  445.2 17.0 %all_to_all.58 = f32[16,1,2080]{2,1,0:T(1,128)S(1)} all-to-all(f32[16,1,2080]{2,1,0:T(1,128)S(1)} %all_to_all.44), channel_id=1, replica_groups=mesh['row'=16,'col'=16] {'col'}, dimensions={0} | all-to-all | bytes 266240 | tf_op jit(solution)/shard_map/all_to_all | solution.py:196
  (200 shorter events, 126.2 us)
Async XLA Ops:
  0.6 11.8 %copy-start = (f32[256,1024]{1,0:T(8,128)S(1)}, f32[256,1024]{1,0:T(8,128)}, u32[]{:S(2)}) copy-start(f32[256,1024]{1,0:T(8,128)} %param.11) | copy-start | bytes 3145732
  2.3 23.0 %all-to-all-start = ((bf16[16,256,64]{1,2,0:T(8,128)(2,1)}), bf16[16,256,64]{1,2,0:T(8,128)(2,1)S(1)}, u32[]{:S(2)}, u32[]{:S(2)}) async-start(bf16[16,256,64]{1,2,0:T(8,128)(2,1)} %broadcast_in_dim.26), calls=%async_computation | async-start | bytes 1048576 | tf_op jit(solution)/shard_map/all_to_all | solution.py:13
  12.4 14.7 %copy-start.8 = (bf16[256,64]{0,1:T(8,128)(2,1)S(1)}, bf16[256,64]{0,1:T(8,128)(2,1)}, u32[]{:S(2)}) copy-start(bf16[256,64]{0,1:T(8,128)(2,1)} %param.8) | copy-start | bytes 98308
  13.1 265.5 %copy-start.11 = (f32[64,256]{1,0:T(8,128)}, f32[64,256]{1,0:T(8,128)S(1)}, u32[]{:S(2)}) copy-start(f32[64,256]{1,0:T(8,128)S(1)} %fusion.47) | copy-start | bytes 196612
  14.1 13.6 %copy-start.13 = (f32[256]{0:T(256)}, f32[256]{0:T(256)S(1)}, u32[]{:S(2)}) copy-start(f32[256]{0:T(256)S(1)} %fusion.87) | copy-start | bytes 3076
  25.3 2.4 copy-start.5
  43.7 5.8 %copy-start.2 = (bf16[65,256,512]{2,1,0:T(8,128)(2,1)}, bf16[65,256,512]{2,1,0:T(8,128)(2,1)S(1)}, u32[]{:S(2)}) copy-start(bf16[65,256,512]{2,1,0:T(8,128)(2,1)S(1)} %pad_maximum_fusion) | copy-start | bytes 51118084
  91.0 33.0 %all-to-all-start.2 = ((f32[16,32,512]{2,1,0:T(8,128)}), f32[16,32,512]{2,1,0:T(8,128)S(1)}, u32[]{:S(2)}, u32[]{:S(2)}) async-start(f32[16,32,512]{2,1,0:T(8,128)} %broadcast_in_dim.29), calls=%async_computation.2 | async-start | bytes 2097152 | tf_op jit(solution)/shard_map/all_to_all | solution.py:13
  126.2 1.0 copy-start.7
  278.2 14.5 %copy-start.6 = (bf16[16,256,64]{1,2,0:T(8,128)(2,1)S(1)}, bf16[16,256,64]{1,2,0:T(8,128)(2,1)}, u32[]{:S(2)}) copy-start(bf16[16,256,64]{1,2,0:T(8,128)(2,1)} %copy-done.5) | copy-start | bytes 1572868
  278.2 14.6 %copy-start.14 = (f32[256]{0:T(256)S(1)}, f32[256]{0:T(256)}, u32[]{:S(2)}) copy-start(f32[256]{0:T(256)} %copy-done.13) | copy-start | bytes 3076
  280.9 36.1 %all-to-all-start.4 = ((f32[16,65,256]{2,1,0:T(8,128)}), f32[16,65,256]{2,1,0:T(8,128)S(1)}, u32[]{:S(2)}, u32[]{:S(2)}) async-start(f32[16,65,256]{2,1,0:T(8,128)} %broadcast_in_dim.31), calls=%async_computation.4 | async-start | bytes 2359296 | tf_op jit(solution)/shard_map/all_to_all | solution.py:13
  318.2 20.1 %all-to-all-start.3 = ((f32[16,1,128]{2,1,0:T(1,128)}), f32[16,1,128]{2,1,0:T(1,128)S(1)}, u32[]{:S(2)}, u32[]{:S(2)}) async-start(f32[16,1,128]{2,1,0:T(1,128)} %broadcast_in_dim.30), calls=%async_computation.3 | async-start | bytes 16384 | tf_op jit(solution)/shard_map/all_to_all | solution.py:13
  326.8 2.2 copy-start.3
  326.9 2.2 copy-start.9
  331.4 6.3 %copy-start.10 = (f32[65,256]{1,0:T(8,128)S(1)}, f32[65,256]{1,0:T(8,128)}, u32[]{:S(2)}) copy-start(f32[65,256]{1,0:T(8,128)} %get-tuple-element.77) | copy-start | bytes 199684
  331.4 22.0 %copy-start.12 = (f32[64,256]{1,0:T(8,128)S(1)}, f32[64,256]{1,0:T(8,128)}, u32[]{:S(2)}) copy-start(f32[64,256]{1,0:T(8,128)} %copy-done.11) | copy-start | bytes 196612
  339.6 13.7 %all-to-all-start.5 = ((f32[16,1,128]{2,1,0:T(1,128)}), f32[16,1,128]{2,1,0:T(1,128)S(1)}, u32[]{:S(2)}, u32[]{:S(2)}) async-start(f32[16,1,128]{2,1,0:T(1,128)} %broadcast_in_dim.33), calls=%async_computation.5 | async-start | bytes 16384 | tf_op jit(solution)/shard_map/all_to_all | solution.py:13
  420.0 2.2 copy-start.4
  432.7 11.1 %all-to-all-start.8 = ((f32[16,1,128]{2,1,0:T(1,128)}), f32[16,1,128]{2,1,0:T(1,128)S(1)}, u32[]{:S(2)}, u32[]{:S(2)}) async-start(f32[16,1,128]{2,1,0:T(1,128)} %broadcast_in_dim.37), calls=%async_computation.8 | async-start | bytes 16384 | tf_op jit(solution)/shard_map/all_to_all | solution.py:13
  444.1 23.4 %copy-start.1 = (f32[256,1024]{1,0:T(8,128)S(1)}, f32[256,1024]{1,0:T(8,128)}, u32[]{:S(2)}) copy-start(f32[256,1024]{1,0:T(8,128)} %param.11) | copy-start | bytes 3145732

commit v2 on v1

v2 whole, which is shorter than its diff:
```python
import math

import jax
import jax.numpy as jnp
from jax import lax
from jax.experimental import pallas as pl
from jax.experimental.pallas import tpu as pltpu
from jax.sharding import PartitionSpec as P

ITERS = 2
NOISE = 0.5
HIGHEST = lax.Precision.HIGHEST


def spread(block, axis, groups=None):
    size = len(groups[0]) if groups else lax.axis_size(axis)
    copies = jnp.broadcast_to(block[None], (size,) + block.shape)
    return lax.all_to_all(copies, axis, 0, 0, axis_index_groups=groups, tiled=True)


def wide_dot(former, latter, dims):
    return lax.dot_general(
        former.astype(jnp.float32),
        latter.astype(jnp.float32),
        ((dims[0:1], dims[1:2]), ((), ())),
        precision=HIGHEST,
        preferred_element_type=jnp.float32,
    )


def half_dot(former, latter, dims):
    return lax.dot_general(
        former,
        latter,
        ((dims[0:1], dims[1:2]), ((), ())),
        preferred_element_type=jnp.float32,
    )


def pivot_table(all_points, pivots):
    count, features = all_points.shape
    owner_ids = pivots // (features + 1)
    component = pivots % (features + 1)
    picks = (owner_ids[:, None] == jnp.arange(count, dtype=jnp.int32)[None, :]).astype(jnp.bfloat16)
    pivot_pts = half_dot(picks, all_points, (1, 0)).astype(jnp.bfloat16)
    valued = (component == 0).astype(jnp.float32)
    unit_dirs = (component[:, None] - 1 == jnp.arange(features, dtype=jnp.int32)[None, :]).astype(
        jnp.bfloat16
    )
    chosen = jnp.sum(pivot_pts.astype(jnp.float32) * unit_dirs.astype(jnp.float32), axis=1)
    return (pivot_pts, valued, unit_dirs, chosen, component[:, None] - 1)


def turned(array, start):
    return lax.dynamic_slice_in_dim(jnp.concatenate([array, array]), start, array.shape[0], 0)


def square_norms(points):
    return jnp.sum(jnp.square(points.astype(jnp.float32)), axis=1)


def pivot_block(pivot_data):
    pivot_pts, valued, unit_dirs, chosen, _ = pivot_data
    norms = square_norms(pivot_pts)
    dots = half_dot(pivot_pts, pivot_pts, (1, 1))
    kernel = jnp.exp(-0.5 * (norms[:, None] + norms[None, :] - 2.0 * dots))
    select = half_dot(pivot_pts, unit_dirs, (1, 1))
    after_terms = select - chosen[None, :]
    before = chosen[:, None] - jnp.transpose(select)
    unit_dots = half_dot(unit_dirs, unit_dirs, (1, 1))
    mixed_terms = (
        valued[:, None] * valued[None, :] + valued[:, None] * after_terms - valued[None, :] * before
    )
    return kernel * (mixed_terms + unit_dots - before * after_terms)


def pair_inverse(first, cross, second):
    scale = 1.0 / (first * second - cross * cross)
    return (second * scale, -cross * scale, first * scale)


def sweep_four(mat, j, lane, sub):
    n = mat.shape[0]
    cols = [jnp.broadcast_to(mat[:, j + q : j + q + 1], mat.shape) for q in range(4)]
    top = (j // 8) * 8

    def entry(p, q):
        return jnp.broadcast_to(cols[q][j + p : j + p + 1, :], (8, n))

    p0, p1, p2 = pair_inverse(entry(0, 0), entry(1, 0), entry(1, 1))
    q00, q01, q10, q11 = entry(2, 0), entry(3, 0), entry(2, 1), entry(3, 1)
    t00, t01 = q00 * p0 + q10 * p1, q00 * p1 + q10 * p2
    t10, t11 = q01 * p0 + q11 * p1, q01 * p1 + q11 * p2
    w00 = entry(2, 2) - (t00 * q00 + t01 * q10)
    w01 = entry(3, 2) - (t10 * q00 + t11 * q10)
    w11 = entry(3, 3) - (t10 * q01 + t11 * q11)
    v0, v1, v2 = pair_inverse(w00, w01, w11)
    s00, s01 = v0 * t00 + v1 * t10, v0 * t01 + v1 * t11
    s10, s11 = v1 * t00 + v2 * t10, v1 * t01 + v2 * t11
    i00 = p0 + (t00 * s00 + t10 * s10)
    i01 = p1 + (t00 * s01 + t10 * s11)
    i11 = p2 + (t01 * s01 + t11 * s11)
    inv = (
        (i00, i01, -s00, -s10),
        (i01, i11, -s01, -s11),
        (-s00, -s01, v0, v1),
        (-s10, -s11, v1, v2),
    )
    inside = (lane >= j) & (lane < j + 4)
    rows = [
        jnp.where(
            inside,
            jnp.where(lane == j + q, 1.0, 0.0),
            jnp.broadcast_to(mat[j + q : j + q + 1, :], (8, n)),
        )
        for q in range(4)
    ]
    pivot_rows = [
        (inv[p][0] * rows[0] + inv[p][1] * rows[1]) + (inv[p][2] * rows[2] + inv[p][3] * rows[3])
        for p in range(4)
    ]
    tiles = []
    for s in range(0, n, 8):
        tile = jnp.where(inside, 0.0, mat[s : s + 8])
        terms = [cols[p][s : s + 8] * pivot_rows[p] for p in range(4)]
        tile = tile - ((terms[0] + terms[1]) + (terms[2] + terms[3]))
        if s == top:
            for p in range(4):
                tile = jnp.where(sub == j - top + p, pivot_rows[p], tile)
        tiles.append(tile)
    return jnp.concatenate(tiles, axis=0)


SWEEP = 128
VMEM = pl.BlockSpec(memory_space=pltpu.VMEM)
SHARE = 32


def inverse_kernel(turn_ref, bands_ref, kpp_ref, out_ref, diag_ref):
    size = out_ref.shape[0]
    bands = size // SHARE
    lane = lax.broadcasted_iota(jnp.int32, (SHARE, 128), 1)
    for k in range(bands):
        packed = bands_ref[k, 2 * SHARE : 2 * SHARE + 8]
        corner = jnp.concatenate(
            [packed] + [pltpu.roll(packed, 128 - SHARE * u, 1) for u in range(1, 4)], axis=0
        )
        band = jnp.concatenate(
            [
                jnp.where(lane < SHARE, 0.5, 1.0) * bands_ref[k, 0:SHARE],
                bands_ref[k, SHARE : 2 * SHARE],
                jnp.where(lane < SHARE, 0.5 * corner, 0.0),
                jnp.zeros((SHARE, size - 384), jnp.float32),
            ],
            axis=1,
        )
        place = pl.multiple_of(lax.rem(k + bands - turn_ref[0], bands) * SHARE, SHARE)
        out_ref[pl.ds(place, SHARE)] = pltpu.roll(band, place, 1)
    out_ref[...] = out_ref[...] + jnp.transpose(out_ref[...]) + NOISE * kpp_ref[...]
    lane = lax.broadcasted_iota(jnp.int32, (8, SWEEP), 1)
    sub = lax.broadcasted_iota(jnp.int32, (8, SWEEP), 0)
    identity = jnp.where(
        lax.broadcasted_iota(jnp.int32, (SWEEP, SWEEP), 0)
        == lax.broadcasted_iota(jnp.int32, (SWEEP, SWEEP), 1),
        1.0,
        0.0,
    )

    def block_step(k, carry):
        here = pl.ds(pl.multiple_of(k * SWEEP, SWEEP), SWEEP)
        diag = out_ref[here, here]
        for j in range(0, SWEEP, 4):
            diag = sweep_four(diag, j, lane, sub)
        diag_ref[...] = diag
        column = out_ref[:, here]
        out_ref[here, here] = identity
        row = jnp.dot(
            diag_ref[...], out_ref[here, :], precision=HIGHEST, preferred_element_type=jnp.float32
        )
        out_ref[:, here] = jnp.zeros((size, SWEEP), jnp.float32)
        out_ref[...] = out_ref[...] - jnp.dot(
            column, row, precision=HIGHEST, preferred_element_type=jnp.float32
        )
        out_ref[here, :] = row
        return carry

    lax.fori_loop(0, size // SWEEP, block_step, 0)


def inverse(turn, bands, kpp):
    vmem = pl.BlockSpec(memory_space=pltpu.VMEM)
    return pl.pallas_call(
        inverse_kernel,
        out_shape=jax.ShapeDtypeStruct(kpp.shape, jnp.float32),
        in_specs=[pl.BlockSpec(memory_space=pltpu.SMEM), vmem, vmem],
        out_specs=vmem,
        scratch_shapes=[pltpu.VMEM((SWEEP, SWEEP), jnp.float32)],
        compiler_params=pltpu.CompilerParams(vmem_limit_bytes=20 * 2**20),
        cost_estimate=pl.CostEstimate(
            flops=10**9, bytes_accessed=3 * 2**20, transcendentals=0
        ),
    )(turn, bands, kpp)


def dot_nt(former, latter):
    return lax.dot_general(
        former, latter, (((1,), (1,)), ((), ())), preferred_element_type=jnp.float32
    )


def thirds_rows(row, count):
    high = row.astype(jnp.bfloat16).astype(jnp.float32)
    middle = (row - high).astype(jnp.bfloat16).astype(jnp.float32)
    low = row - high - middle
    sub = lax.broadcasted_iota(jnp.int32, (count, row.shape[1]), 0)
    parts = jnp.where(
        sub == 0, high, jnp.where(sub == 1, middle, jnp.where(sub == 2, low, jnp.zeros_like(low)))
    )
    return parts.astype(jnp.bfloat16)


def plain_rows(m, u, columns, turned_ref, lead):
    return (columns[:, u : u + 1] - turned_ref[pl.ds(m, 1)]) * lead


def each_dimension(pivots_ref, columns_ref, features, start, body):
    columns_ref[:, 0:features] = pivots_ref[...].astype(jnp.float32)

    def group(step, carry):
        columns = columns_ref[...]
        for u in range(UNROLL):
            carry = body(step * UNROLL + u, u, columns, carry)
        columns_ref[...] = pltpu.roll(columns, columns.shape[1] - UNROLL, 1)
        return carry

    return lax.fori_loop(0, features // UNROLL, group, start)


def factor_kernel(
    pivots_ref, dirs_ref, comp_ref, points_ref, turned_ref, field_ref,
    lead_ref, extra_ref, sums_ref, kern_ref, comps_ref, total_ref, columns_ref,
):
    features = turned_ref.shape[0]
    rank = lead_ref.shape[0]

    def add(rows, line):
        left = jnp.concatenate([rows[:SHARE], thirds_rows(line, 16)], axis=0)
        total_ref[...] += dot_nt(left, rows)

    pivot_pts = pivots_ref[...]
    wide_pts = pivot_pts.astype(jnp.float32)
    wide_dirs = dirs_ref[...].astype(jnp.float32)
    norms = jnp.sum(wide_pts * wide_pts, axis=1, keepdims=True)
    chosen = jnp.sum(wide_pts * wide_dirs, axis=1, keepdims=True)
    valued = jnp.where(comp_ref[...] < 0, 1.0, 0.0)
    own_norms = jnp.sum(turned_ref[...] * turned_ref[...], axis=0, keepdims=True)
    dots = dot_nt(pivot_pts, points_ref[...])
    kern = jnp.exp(-0.5 * (own_norms + norms - 2.0 * dots))
    along = dot_nt(dirs_ref[...], points_ref[...]) - chosen
    lead = kern * (valued + along)
    kern_ref[...] = kern
    lead_ref[...] = lead
    plain = -along * lead
    extra = (kern + plain).astype(jnp.bfloat16).astype(jnp.float32) - plain.astype(
        jnp.bfloat16
    ).astype(jnp.float32)
    extra_ref[...] = jnp.where(comp_ref[...] < 0, 0.0, extra)
    comps_ref[...] = jnp.broadcast_to(comp_ref[...], comps_ref.shape)
    total_ref[...] = jnp.zeros_like(total_ref)
    add(lead.astype(jnp.bfloat16), field_ref[features : features + 1])

    def body(m, u, columns, carry):
        plain = plain_rows(m, u, columns, turned_ref, lead_ref[...])
        rows = jnp.where(comps_ref[...] == m, kern_ref[...] + plain, plain)
        add(rows.astype(jnp.bfloat16), field_ref[pl.ds(m, 1)])
        return carry

    each_dimension(pivots_ref, columns_ref, features, 0, body)
    sums_ref[0:SHARE] = total_ref[0:SHARE, 0:128]
    sums_ref[SHARE : 2 * SHARE] = total_ref[0:SHARE, 128:256]
    lane = lax.broadcasted_iota(jnp.int32, (8, 128), 1)
    corner = jnp.zeros((8, 128), jnp.float32)
    for u in range(4):
        piece = total_ref[8 * u : 8 * u + 8, 256:384]
        piece = pltpu.roll(piece, SHARE * u, 1) if u else piece
        corner = jnp.where((lane >= SHARE * u) & (lane < SHARE * (u + 1)), piece, corner)
    sums_ref[2 * SHARE : 2 * SHARE + 8] = corner
    high = total_ref[SHARE : SHARE + 1]
    full = high + (total_ref[SHARE + 1 : SHARE + 2] + total_ref[SHARE + 2 : SHARE + 3])
    for u in range(rank // 128):
        sums_ref[72 + u : 73 + u] = high[:, 128 * u : 128 * u + 128]
        sums_ref[76 + u : 77 + u] = full[:, 128 * u : 128 * u + 128]
    field = field_ref[0 : features + 1]
    square = jnp.sum(jnp.sum(field * field, axis=0, keepdims=True), axis=1, keepdims=True)
    sums_ref[80:88] = jnp.broadcast_to(square, (8, 128))


UNROLL = 8


def make_factor(pivot_data, points, turned_points, field):
    pivot_pts, comp, dirs = pivot_data
    rank, features = pivot_pts.shape
    count = points.shape[0]
    return pl.pallas_call(
        factor_kernel,
        in_specs=[VMEM] * 6,
        out_specs=[VMEM] * 3,
        out_shape=[
            jax.ShapeDtypeStruct((rank, count), jnp.float32),
            jax.ShapeDtypeStruct((rank, count), jnp.float32),
            jax.ShapeDtypeStruct((88, 128), jnp.float32),
        ],
        scratch_shapes=[
            pltpu.VMEM((rank, count), jnp.float32),
            pltpu.VMEM((rank, count), jnp.int32),
            pltpu.VMEM((SHARE + 16, rank), jnp.float32),
            pltpu.VMEM((rank, 128), jnp.float32),
        ],
        compiler_params=pltpu.CompilerParams(vmem_limit_bytes=20 * 2**20),
        cost_estimate=pl.CostEstimate(
            flops=2 * 48 * 65 * rank * count, bytes_accessed=4 * 2**20, transcendentals=rank * count
        ),
    )(pivot_pts, dirs, comp, points, turned_points, field)


def descend_kernel(
    pivots_ref, turned_ref, lead_ref, extra_ref, picks_ref, inv_ref, sums_ref, field_ref, old_ref,
    gamma_ref, out_ref, new_gamma_ref, coef_ref, columns_ref,
):
    features = field_ref.shape[0] - 1
    lines = sums_ref[...]
    low = jnp.concatenate([lines[u : u + 1] for u in range(4)], axis=1)
    full = jnp.concatenate([lines[u : u + 1] for u in range(4, 8)], axis=1)
    coef = jnp.dot(
        jnp.broadcast_to(low, (8, low.shape[1])),
        inv_ref[...],
        precision=HIGHEST,
        preferred_element_type=jnp.float32,
    )[0:1]
    coef_ref[...] = thirds_rows(coef, 16)
    gamma = (lines[8:9, 0:1] - jnp.sum(full * coef, axis=1, keepdims=True)) / NOISE
    new_gamma_ref[...] = jnp.broadcast_to(gamma, (8, 128))
    beta = gamma / gamma_ref[0:1, 0:1]

    def apply(rows):
        parts = jnp.dot(
            coef_ref[...], rows.astype(jnp.bfloat16), preferred_element_type=jnp.float32
        )
        return parts[0:1] + (parts[1:2] + parts[2:3])

    out_ref[features : features + 1] = apply(lead_ref[...])
    out_ref[0:features] = jnp.dot(
        picks_ref[...].astype(jnp.float32) * coef,
        extra_ref[...],
        precision=HIGHEST,
        preferred_element_type=jnp.float32,
    )

    def body(m, u, columns, carry):
        out_ref[pl.ds(m, 1)] += apply(plain_rows(m, u, columns, turned_ref, lead_ref[...]))
        return carry

    each_dimension(pivots_ref, columns_ref, features, 0, body)
    out_ref[...] = (field_ref[...] - out_ref[...]) / NOISE + beta * old_ref[...]


def descend(factor, inv, sums, field, old, gamma):
    rank, count = factor[2].shape
    return pl.pallas_call(
        descend_kernel,
        in_specs=[VMEM] * 10,
        out_specs=[VMEM] * 2,
        out_shape=[
            jax.ShapeDtypeStruct(field.shape, jnp.float32),
            jax.ShapeDtypeStruct((8, 128), jnp.float32),
        ],
        scratch_shapes=[pltpu.VMEM((16, rank), jnp.bfloat16), pltpu.VMEM((rank, 128), jnp.float32)],
        compiler_params=pltpu.CompilerParams(vmem_limit_bytes=20 * 2**20),
        cost_estimate=pl.CostEstimate(
            flops=2 * 16 * 65 * rank * count, bytes_accessed=5 * 2**20, transcendentals=0
        ),
    )(*factor, inv, sums, field, old, gamma)


def project_kernel(
    pivots_ref, turned_ref, lead_ref, extra_ref, picks_ref, image_ref, field_ref, curve_ref,
    gamma_ref, next_ref, sums_ref, step_ref, columns_ref,
):
    features = field_ref.shape[0] - 1
    curve = curve_ref[0, 0:1, 0:1]
    for k in range(1, curve_ref.shape[0]):
        curve = curve + curve_ref[k, 0:1, 0:1]
    scale = gamma_ref[0:1, 0:1] / curve
    step_ref[...] = jnp.broadcast_to(scale, (8, 128))
    next_ref[...] = field_ref[...] - scale * image_ref[...]

    def add(line, rows):
        return dot_nt(thirds_rows(line, 16), rows.astype(jnp.bfloat16))

    total = add(next_ref[features : features + 1], lead_ref[...])

    def body(m, u, columns, total):
        rows = plain_rows(m, u, columns, turned_ref, lead_ref[...])
        return total + add(next_ref[pl.ds(m, 1)], rows)

    total = each_dimension(pivots_ref, columns_ref, features, total, body)
    field = next_ref[...]
    upper = field[0:features].astype(jnp.bfloat16)
    rest = field[0:features] - upper.astype(jnp.float32)
    middle = rest.astype(jnp.bfloat16)
    lower = (rest - middle.astype(jnp.float32)).astype(jnp.bfloat16)

    def meet(part):
        return lax.dot_general(
            picks_ref[...], part, (((0,), (0,)), ((), ())), preferred_element_type=jnp.float32
        )

    first = meet(upper)
    ones = jnp.ones((8, field.shape[1]), jnp.float32)
    both = [
        lax.dot_general(
            ones,
            extra_ref[...] * part,
            (((1,), (1,)), ((), ())),
            precision=HIGHEST,
            preferred_element_type=jnp.float32,
        )[0:1]
        for part in (first, first + (meet(middle) + meet(lower)))
    ]
    high = total[0:1] + both[0]
    full = total[0:1] + (total[1:2] + total[2:3]) + both[1]
    for u in range(high.shape[1] // 128):
        sums_ref[u : 1 + u] = high[:, 128 * u : 128 * u + 128]
        sums_ref[4 + u : 5 + u] = full[:, 128 * u : 128 * u + 128]
    square = jnp.sum(jnp.sum(field * field, axis=0, keepdims=True), axis=1, keepdims=True)
    sums_ref[8:16] = jnp.broadcast_to(square, (8, 128))


def project(factor, image, field, curve, gamma):
    rank, count = factor[2].shape
    return pl.pallas_call(
        project_kernel,
        in_specs=[VMEM] * 9,
        out_specs=[VMEM] * 3,
        out_shape=[
            jax.ShapeDtypeStruct(field.shape, jnp.float32),
            jax.ShapeDtypeStruct((16, 128), jnp.float32),
            jax.ShapeDtypeStruct((8, 128), jnp.float32),
        ],
        scratch_shapes=[pltpu.VMEM((rank, 128), jnp.float32)],
        compiler_params=pltpu.CompilerParams(vmem_limit_bytes=20 * 2**20),
        cost_estimate=pl.CostEstimate(
            flops=2 * 16 * 65 * rank * count, bytes_accessed=4 * 2**20, transcendentals=0
        ),
    )(*factor, image, field, curve, gamma)


def image_kernel(fields_ref, row_points_ref, col_points_ref, image_ref):
    blocks, width, count = fields_ref.shape
    features = width - 1

    def dot(former, latter):
        return jnp.dot(former, latter, preferred_element_type=jnp.float32)

    sides = []
    for k in range(blocks):
        points = col_points_ref[k]
        spare = jnp.zeros((count, features), jnp.float32)
        wide = jnp.concatenate([points.astype(jnp.float32), spare], axis=1)
        turned_points = jnp.transpose(wide)[0:features]
        lane = lax.broadcasted_iota(jnp.int32, wide.shape, 1)
        with_ones = jnp.where(lane == features, 1.0, wide).astype(jnp.bfloat16)
        slopes = fields_ref[k, 0:features]
        owned = fields_ref[k, features : features + 1] - jnp.sum(
            turned_points * slopes, axis=0, keepdims=True
        )
        norms = jnp.sum(turned_points * turned_points, axis=0, keepdims=True)
        high = slopes.astype(jnp.bfloat16)
        rest = slopes - high.astype(jnp.float32)
        middle = rest.astype(jnp.bfloat16)
        low = (rest - middle.astype(jnp.float32)).astype(jnp.bfloat16)
        sides.append((with_ones, owned, norms, high, middle, low))

    def rows(j, carry):
        points = row_points_ref[j]
        wide = points.astype(jnp.float32)
        own_norms = jnp.sum(wide * wide, axis=1, keepdims=True)
        thrice = jnp.concatenate([points] * 3, axis=1)
        total = jnp.zeros((count, 2 * features), jnp.float32)
        base = jnp.zeros((count, 2 * features), jnp.float32)
        for k in range(blocks):
            with_ones, owned, norms, high, middle, low = sides[k]
            dots = dot_nt(points, col_points_ref[k])
            kern = jnp.exp(-0.5 * (own_norms + norms - 2.0 * dots))
            cross = dot(thrice, jnp.concatenate([high, middle, low], axis=0))
            weight = kern * (cross + owned)
            upper = weight.astype(jnp.bfloat16)
            lower = (weight - upper.astype(jnp.float32)).astype(jnp.bfloat16)
            total += dot(upper, with_ones) + dot(lower, with_ones)
            upper = kern.astype(jnp.bfloat16)
            lower = (kern - upper.astype(jnp.float32)).astype(jnp.bfloat16)
            base += dot_nt(upper, jnp.concatenate([high, middle], axis=0)) + dot_nt(
                lower, jnp.concatenate([high, jnp.zeros_like(high)], axis=0)
            )
        value = total[:, features : features + 1]
        spare = jnp.zeros((count, features), jnp.float32)
        total += jnp.concatenate(
            [base[:, 0:features] + base[:, features:] - wide * value, spare], axis=1
        )
        image_ref[j] = jnp.transpose(total)[0:width]
        return carry

    lax.fori_loop(0, row_points_ref.shape[0], rows, 0)


def image_part(fields, row_points, col_points):
    blocks, width, count = fields.shape
    return pl.pallas_call(
        image_kernel,
        in_specs=[VMEM] * 3,
        out_specs=VMEM,
        out_shape=jax.ShapeDtypeStruct((row_points.shape[0], width, count), jnp.float32),
        compiler_params=pltpu.CompilerParams(vmem_limit_bytes=24 * 2**20),
        cost_estimate=pl.CostEstimate(
            flops=2 * 5 * blocks * blocks * count * count * 128,
            bytes_accessed=2**20,
            transcendentals=blocks * blocks * count * count,
        ),
    )(fields, row_points, col_points)


def gather_kernel(parts_ref, own_ref, image_ref, curve_ref):
    image = NOISE * own_ref[...]
    for k in range(parts_ref.shape[0]):
        image = image + parts_ref[k]
    image_ref[...] = image
    curve = jnp.sum(own_ref[...] * image, axis=0, keepdims=True)
    curve_ref[...] = jnp.broadcast_to(
        jnp.sum(curve, axis=1, keepdims=True)[None], curve_ref.shape
    )


def gather_image(parts, own, devices):
    return pl.pallas_call(
        gather_kernel,
        in_specs=[VMEM] * 2,
        out_specs=[VMEM] * 2,
        out_shape=[
            jax.ShapeDtypeStruct(own.shape, jnp.float32),
            jax.ShapeDtypeStruct((devices, 8, 128), jnp.float32),
        ],
    )(parts, own)


def advance_kernel(curve_ref, gamma_ref, sides_ref, moves_ref, out_ref):
    curve = curve_ref[0, 0:1, 0:1]
    for k in range(1, curve_ref.shape[0]):
        curve = curve + curve_ref[k, 0:1, 0:1]
    scale = gamma_ref[0:1, 0:1] / curve
    out_ref[0] = sides_ref[0] + scale * moves_ref[0]
    out_ref[1] = sides_ref[1] - scale * moves_ref[1]


def local(points, pivots, right_values, right_derivs):
    row, col = lax.axis_index("row"), lax.axis_index("col")
    row_count, col_count = lax.axis_size("row"), lax.axis_size("col")
    row_total, features = points.shape
    samples = right_values.shape[1]
    width = features + 1

    side = math.isqrt(row_count)
    by_high = [[high * side + low for high in range(side)] for low in range(side)]
    by_low = [[high * side + low for low in range(side)] for high in range(side)]
    point_blocks = spread(points, "row")
    grid_blocks = point_blocks.reshape((side, side) + points.shape)
    row_points = lax.dynamic_index_in_dim(grid_blocks, row // side, 0, keepdims=False)
    col_points = lax.dynamic_index_in_dim(grid_blocks, row % side, 1, keepdims=False)
    all_points = point_blocks.reshape(-1, features)
    lanes = jnp.arange(samples * features, dtype=jnp.int32)
    picks = (lanes[None, :] == jnp.arange(features, dtype=jnp.int32)[:, None] * samples + col)
    value_picks = (jnp.arange(samples, dtype=jnp.int32) == col)[None, :]
    residual = jnp.concatenate(
        [wide_dot(picks, right_derivs, (1, 1)), wide_dot(value_picks, right_values, (1, 1))],
        axis=0,
    )

    pivot_data = pivot_table(all_points, turned(pivots, col * SHARE))
    own_turned = jnp.transpose(points.astype(jnp.float32))
    rank = pivots.shape[0]
    lead, extra, sums = make_factor(
        (pivot_data[0], pivot_data[4], pivot_data[2]), points, own_turned, residual
    )
    factor = (pivot_data[0], own_turned, lead, extra, jnp.transpose(pivot_data[2]))
    sums = jnp.sum(spread(jnp.sum(spread(sums, "row", by_high), axis=0), "row", by_low), axis=0)
    inv = inverse(col[None], spread(sums[:72], "col"), pivot_block(pivot_data))

    gamma = jnp.ones((8, 128), jnp.float32)
    direction, gamma = descend(
        factor, inv, sums[72:], residual, jnp.zeros_like(residual), gamma
    )
    estimate = jnp.zeros_like(residual)
    for iteration in range(ITERS):
        fields = spread(direction, "row", by_high)
        parts = lax.all_to_all(
            image_part(fields, row_points, col_points),
            "row", 0, 0, axis_index_groups=by_low, tiled=True,
        )
        image, curve = gather_image(parts, direction, row_count)
        curve = lax.all_to_all(curve, "row", 0, 0, tiled=True)
        if iteration + 1 < ITERS:
            residual, sums, step = project(factor, image, residual, curve, gamma)
            estimate = step[0, 0] * direction
            sums = jnp.sum(spread(sums, "row"), axis=0)
            direction, gamma = descend(factor, inv, sums, residual, direction, gamma)
    fields = pl.pallas_call(
        advance_kernel,
        in_specs=[VMEM] * 4,
        out_specs=VMEM,
        out_shape=jax.ShapeDtypeStruct((2, width, row_total), jnp.float32),
    )(curve, gamma, jnp.stack([estimate, residual]), jnp.stack([direction, image]))
    share_rows = row_total // col_count
    fields = fields.reshape(2, width, col_count, share_rows)
    fields = jnp.transpose(fields, (2, 0, 1, 3)).reshape(col_count, -1)
    fields = lax.all_to_all(fields, "col", 0, 0, tiled=True)
    fields = jnp.transpose(fields.reshape(samples, 2, width, share_rows), (1, 3, 2, 0))
    values = fields[:, :, features]
    derivs = fields[:, :, :features].reshape(2, share_rows, features * samples)
    return (values[0], derivs[0], values[1], derivs[1])


def solution(mesh):
    in_specs = (P("row", None), P(), P("row", None), P("row", None))
    out_specs = (P(("row", "col"), None),) * 4
    return jax.shard_map(local, mesh=mesh, in_specs=in_specs, out_specs=out_specs, check_vma=False)
```

time: 476 us -> 288 us (0.61); the launches traced: 468 us -> 287 us
  other arithmetic: 145 us -> 5.14 us
  Pallas kernels: 0 us -> 89.1 us
  matrix products: 75.6 us -> 7.31 us
  blocking collectives: 93.9 us -> 71.1 us
  waiting for transfers between devices: 58.8 us -> 37.1 us
  starting transfers between devices: 52 us -> 38.9 us
  between operations: 6.61 us -> 1.02 us
    another operation x25 -> x3, other arithmetic: 127 us -> 2.91 us  [the longest x1 1.58 us: local(): jnp.stack([direction, image])]
    pallas_call x0 -> x10, Pallas kernels: none -> 89.1 us  [the longest x1 39.3 us: inverse(): pl.pallas_call(inverse_kernel, out_shape=jax.ShapeDtypeStruct(kpp.shape,...]
    dot_general x12 -> x4, matrix products: 45.6 us -> 6.5 us  [half_dot(): lax.dot_general(former, latter, ((dims[0:1], dims[1:2]), ((), ())), prefe...]
    all_to_all x3 -> x5, blocking collectives: 76.9 us -> 50.3 us  [the longest x3 28.2 us: spread(): lax.all_to_all(copies, axis, 0, 0, axis_index_groups=groups, tiled=True)]
    all_to_all x6, waiting for transfers between devices: 58.8 us -> 37.1 us  [the longest x4 27.1 us: spread(): lax.all_to_all(copies, axis, 0, 0, axis_index_groups=groups, tiled=True)]
    dot_general x8 -> x2, matrix products: 18.8 us -> 0.8 us  [wide_dot(): lax.dot_general(former.astype(jnp.float32), latter.astype(jnp.float32), (...]
    all_to_all x6, starting transfers between devices: 52 us -> 38.9 us  [the longest x4 31.4 us: spread(): lax.all_to_all(copies, axis, 0, 0, axis_index_groups=groups, tiled=True)]
    another operation x34 -> x0, matrix products: 11.3 us -> none  [the longest x6 5.47 us: local(): chol = jnp.linalg.cholesky(NOISE * pivot_block(pivot_data) + gram)]
  transfers between devices with their start and end apart: 6 -> 6, of which waited for: 5 -> 6; matrix products, arithmetic and copies ran while one was open for 5% -> 7% of each run, Pallas kernels for 0% -> 0%
where the time goes in v2:
time: 288 us; the launch traced here: 287 us
  Pallas kernels  89.1 us (31%)
  blocking collectives  71.1 us (25%)
  starting transfers between devices  38.9 us (14%)
  waiting for transfers between devices  37.1 us (13%)
  local copies, waits for them, and re-layouts  36.9 us (13%)
  matrix products  7.31 us (3%)
  other arithmetic  5.14 us (2%)
    pallas_call x1, Pallas kernels, inverse(): pl.pallas_call(inverse_kernel, out_shape=jax.ShapeDtypeStruct(kpp.shape,...  39.3 us
    all_to_all x4, starting transfers between devices, spread(): lax.all_to_all(copies, axis, 0, 0, axis_index_groups=groups, tiled=True)  31.4 us
    all_to_all x3, blocking collectives, spread(): lax.all_to_all(copies, axis, 0, 0, axis_index_groups=groups, tiled=True)  28.2 us
    all_to_all x4, waiting for transfers between devices, spread(): lax.all_to_all(copies, axis, 0, 0, axis_index_groups=groups, tiled=True)  27.1 us
    all_to_all x1, blocking collectives, local(): fields = lax.all_to_all(fields, 'col', 0, 0, tiled=True)  20.8 us
    unnamed x59, local copies, waits for them, and re-layouts  16 us
    pallas_call x2, Pallas kernels, descend(): pl.pallas_call(descend_kernel, in_specs=[VMEM] * 10, out_specs=[VMEM] * 2...  14.4 us
    pallas_call x2, Pallas kernels, image_part(): pl.pallas_call(image_kernel, in_specs=[VMEM] * 3, out_specs=VMEM, out_sha...  13.6 us
  transfers between devices with their start and end apart: 6, of which 6 were waited for; matrix products, arithmetic and copies ran while one was open for 7% of the time, Pallas kernels for 0%

profile of v2, /device:TPU:1, one launch (start us, length us, event | category | flops | bytes accessed | tf_op | source)
XLA Modules:
  0.0 286.5 jit_solution(13161801231721085966)
XLA Ops:
  2.4 9.2 %all-to-all-start = ((bf16[16,256,64]{1,2,0:T(8,128)(2,1)}), bf16[16,256,64]{1,2,0:T(8,128)(2,1)S(1)}, u32[]{:S(2)}, u32[]{:S(2)}) async-start(bf16[16,256,64]{1,2,0:T(8,128)(2,1)} %broadcast_in_dim.22), calls=%async_computation | async-start | bytes 1048576 | tf_op jit(solution)/shard_map/all_to_all | solution.py:18
  13.0 12.4 %all-to-all-done = bf16[16,256,64]{1,2,0:T(8,128)(2,1)S(1)} async-done(((bf16[16,256,64]{1,2,0:T(8,128)(2,1)}), bf16[16,256,64]{1,2,0:T(8,128)(2,1)S(1)}, u32[]{:S(2)}, u32[]{:S(2)}) %all-to-all-start) | async-done | bytes 524320 | tf_op jit(solution)/shard_map/all_to_all | solution.py:18
  27.0 9.0 %shard_map.75 = (f32[512,256]{1,0:T(8,128)S(1)}, f32[512,256]{1,0:T(8,128)S(1)}, f32[88,128]{1,0:T(8,128)S(1)}) custom-call(bf16[512,64]{1,0:T(8,128)(2,1)S(1)} %get-tuple-element.52.pivots_ref, bf16[512,64]{1,0:T(8,128)(2,1)S(1)} %fusion.12.dirs_ref, s32[512,1]{1,0:T(8,128)S(1)} %copy.57.comp_ref, bf16[256,64]{1,0:T(8,128)(2,1)S(1)} %copy.58.points_ref, ...), custom_call_target="tpu_custom_call" | custom-call | flops 817889280 | bytes 4194304 | tf_op jit(solution)/shard_map/pallas_call | solution.py:305
  36.0 9.8 %all_to_all.65 = f32[4,88,128]{2,1,0:T(8,128)S(1)} all-to-all(f32[4,88,128]{2,1,0:T(8,128)S(1)} %broadcast_in_dim.24), channel_id=1, replica_groups={{0,64,128,192},{16,80,144,208},{32,96,160,224},{48,112,176,240},{1,65,1..., dimensions={0} | all-to-all | bytes 360448 | tf_op jit(solution)/shard_map/all_to_all | solution.py:18
  45.8 7.5 %all_to_all.66 = f32[4,88,128]{2,1,0:T(8,128)S(1)} all-to-all(f32[4,88,128]{2,1,0:T(8,128)S(1)} %broadcast_in_dim.25), channel_id=1, replica_groups={{0,16,32,48},{64,80,96,112},{128,144,160,176},{192,208,224,240},{1,17,3..., dimensions={0} | all-to-all | bytes 360448 | tf_op jit(solution)/shard_map/all_to_all | solution.py:18
  54.2 12.4 %all-to-all-start.3 = ((f32[16,72,128]{2,1,0:T(8,128)}), f32[16,72,128]{2,1,0:T(8,128)S(1)}, u32[]{:S(2)}, u32[]{:S(2)}) async-start(f32[16,72,128]{2,1,0:T(8,128)} %broadcast_in_dim.26), calls=%async_computation.3 | async-start | bytes 1179648 | tf_op jit(solution)/shard_map/all_to_all | solution.py:18
  74.7 8.6 %all-to-all-done.3.bands_ref = f32[16,72,128]{2,1,0:T(8,128)S(1)} async-done(((f32[16,72,128]{2,1,0:T(8,128)}), f32[16,72,128]{2,1,0:T(8,128)S(1)}, u32[]{:S(2)}, u32[]{:S(2)}) %all-to-all-start.3) | async-done | bytes 589856 | tf_op jit(solution)/shard_map/all_to_all | solution.py:18
  86.4 39.3 %shard_map.76.inv_ref = f32[512,512]{1,0:T(8,128)S(1)} custom-call(s32[1]{0:T(128)} %bitcast.4.turn_ref, f32[16,72,128]{2,1,0:T(8,128)S(1)} %copy-done.6, f32[512,512]{1,0:T(8,128)S(1)} %copy-done.3), custom_call_target="tpu_custom_call" | custom-call | flops 1000000000 | bytes 3145728 | tf_op jit(solution)/shard_map/pallas_call | solution.py:192
  125.7 7.2 %shard_map.77 = (f32[65,256]{1,0:T(8,128)S(1)}, f32[8,128]{1,0:T(8,128)S(1)}) custom-call(bf16[512,64]{1,0:T(8,128)(2,1)S(1)} %get-tuple-element.52.pivots_ref, f32[64,256]{1,0:T(8,128)S(1)} %convert_bitcast_fusion.turned_ref, f32[512,256]{1,0:T(8,128)S(1)} %get-tuple-element.18.lead_ref, f32[512,256]{1,0:T(8,128)S(1)} %get-tuple-element.19.extra_ref, ...), custom_call_target="tpu_custom_call" | custom-call | flops 272629760 | bytes 5242880 | tf_op jit(solution)/shard_map/pallas_call | solution.py:370
  134.3 6.3 %all-to-all-start.4 = ((f32[4,65,256]{2,1,0:T(8,128)}), f32[4,65,256]{2,1,0:T(8,128)}, u32[]{:S(2)}, u32[]{:S(2)}) async-start(f32[4,65,256]{2,1,0:T(8,128)} %broadcast_in_dim.29), calls=%async_computation.4 | async-start | bytes 589824 | tf_op jit(solution)/shard_map/all_to_all | solution.py:18
  150.6 6.9 %shard_map.78 = f32[4,65,256]{2,1,0:T(8,128)S(1)} custom-call(f32[4,65,256]{2,1,0:T(8,128)} %all-to-all-done.4.fields_ref, bf16[4,256,64]{2,1,0:T(8,128)(2,1)S(1)} %bitcast.48, bf16[4,256,64]{2,1,0:T(8,128)(2,1)S(1)} %bitcast.46), custom_call_target="tpu_custom_call" | custom-call | flops 1342177280 | bytes 1048576 | tf_op jit(solution)/shard_map/pallas_call | solution.py:519
  157.6 8.8 %all_to_all.67.parts_ref = f32[4,65,256]{2,1,0:T(8,128)} all-to-all(f32[4,65,256]{2,1,0:T(8,128)S(1)} %shard_map.78), channel_id=1, replica_groups={{0,16,32,48},{64,80,96,112},{128,144,160,176},{192,208,224,240},{1,17,3..., dimensions={0} | all-to-all | bytes 532480 | tf_op jit(solution)/shard_map/all_to_all | solution.py:605
  168.1 13.3 %all_to_all.68.curve_ref = f32[16,8,128]{2,1,0:T(8,128)S(1)} all-to-all(f32[16,8,128]{2,1,0:T(8,128)} %get-tuple-element.23), channel_id=1, replica_groups=mesh['row'=16,'col'=16] {'row'}, dimensions={0} | all-to-all | bytes 131072 | tf_op jit(solution)/shard_map/all_to_all | solution.py:610
  183.0 7.6 %shard_map.80 = (f32[65,256]{1,0:T(8,128)S(1)}, f32[16,128]{1,0:T(8,128)S(1)}, f32[8,128]{1,0:T(8,128)S(1)}) custom-call(bf16[512,64]{1,0:T(8,128)(2,1)S(1)} %get-tuple-element.52.pivots_ref, f32[64,256]{1,0:T(8,128)S(1)} %convert_bitcast_fusion.turned_ref, f32[512,256]{1,0:T(8,128)S(1)} %get-tuple-element.18.lead_ref, ...), custom_call_target="tpu_custom_call" | custom-call | flops 272629760 | bytes 4194304 | tf_op jit(solution)/shard_map/pallas_call | solution.py:442
  191.8 11.0 %all_to_all.69 = f32[16,16,128]{2,1,0:T(8,128)} all-to-all(f32[16,16,128]{2,1,0:T(8,128)S(1)} %broadcast_in_dim.30), channel_id=1, replica_groups=mesh['row'=16,'col'=16] {'row'}, dimensions={0} | all-to-all | bytes 262144 | tf_op jit(solution)/shard_map/all_to_all | solution.py:18
  206.6 7.2 %shard_map.81 = (f32[65,256]{1,0:T(8,128)S(1)}, f32[8,128]{1,0:T(8,128)S(1)}) custom-call(bf16[512,64]{1,0:T(8,128)(2,1)S(1)} %get-tuple-element.52.pivots_ref, f32[64,256]{1,0:T(8,128)S(1)} %convert_bitcast_fusion.turned_ref, f32[512,256]{1,0:T(8,128)S(1)} %get-tuple-element.18.lead_ref, f32[512,256]{1,0:T(8,128)S(1)} %get-tuple-element.19.extra_ref, ...), custom_call_target="tpu_custom_call" | custom-call | flops 272629760 | bytes 5242880 | tf_op jit(solution)/shard_map/pallas_call | solution.py:370
  215.2 3.5 %all-to-all-start.8 = ((f32[4,65,256]{2,1,0:T(8,128)}), f32[4,65,256]{2,1,0:T(8,128)S(1)}, u32[]{:S(2)}, u32[]{:S(2)}) async-start(f32[4,65,256]{2,1,0:T(8,128)} %broadcast_in_dim.31), calls=%async_computation.8 | async-start | bytes 589824 | tf_op jit(solution)/shard_map/all_to_all | solution.py:18
  219.8 4.7 %all-to-all-done.8.fields_ref = f32[4,65,256]{2,1,0:T(8,128)S(1)} async-done(((f32[4,65,256]{2,1,0:T(8,128)}), f32[4,65,256]{2,1,0:T(8,128)S(1)}, u32[]{:S(2)}, u32[]{:S(2)}) %all-to-all-start.8) | async-done | bytes 266272 | tf_op jit(solution)/shard_map/all_to_all | solution.py:18
  226.4 6.7 %shard_map.82 = f32[4,65,256]{2,1,0:T(8,128)} custom-call(f32[4,65,256]{2,1,0:T(8,128)S(1)} %all-to-all-done.8.fields_ref, bf16[4,256,64]{2,1,0:T(8,128)(2,1)S(1)} %bitcast.49, bf16[4,256,64]{2,1,0:T(8,128)(2,1)S(1)} %bitcast.47), custom_call_target="tpu_custom_call" | custom-call | flops 1342177280 | bytes 1048576 | tf_op jit(solution)/shard_map/pallas_call | solution.py:519
  233.1 3.6 %all-to-all-start.9 = ((f32[4,65,256]{2,1,0:T(8,128)}), f32[4,65,256]{2,1,0:T(8,128)S(1)}, u32[]{:S(2)}, u32[]{:S(2)}) async-start(f32[4,65,256]{2,1,0:T(8,128)} %shard_map.82), calls=%async_computation.9 | async-start | bytes 589824 | tf_op jit(solution)/shard_map/all_to_all | solution.py:605
  237.3 5.0 %all-to-all-done.9.parts_ref = f32[4,65,256]{2,1,0:T(8,128)S(1)} async-done(((f32[4,65,256]{2,1,0:T(8,128)}), f32[4,65,256]{2,1,0:T(8,128)S(1)}, u32[]{:S(2)}, u32[]{:S(2)}) %all-to-all-start.9) | async-done | bytes 266272 | tf_op jit(solution)/shard_map/all_to_all | solution.py:605
  244.8 4.0 %all-to-all-start.10 = ((f32[16,8,128]{2,1,0:T(8,128)}), f32[16,8,128]{2,1,0:T(8,128)S(1)}, u32[]{:S(2)}, u32[]{:S(2)}) async-start(f32[16,8,128]{2,1,0:T(8,128)} %get-tuple-element.28), calls=%async_computation.10 | async-start | bytes 131072 | tf_op jit(solution)/shard_map/all_to_all | solution.py:610
  251.0 5.0 %all-to-all-done.10.curve_ref = f32[16,8,128]{2,1,0:T(8,128)S(1)} async-done(((f32[16,8,128]{2,1,0:T(8,128)}), f32[16,8,128]{2,1,0:T(8,128)S(1)}, u32[]{:S(2)}, u32[]{:S(2)}) %all-to-all-start.10) | async-done | bytes 65568 | tf_op jit(solution)/shard_map/all_to_all | solution.py:610
  260.4 20.8 %all_to_all.70 = f32[16,1,2080]{2,1,0:T(1,128)S(1)} all-to-all(f32[16,1,2080]{2,1,0:T(1,128)S(1)} %all_to_all.52), channel_id=1, replica_groups=mesh['row'=16,'col'=16] {'col'}, dimensions={0} | all-to-all | bytes 266240 | tf_op jit(solution)/shard_map/all_to_all | solution.py:625
  (113 shorter events, 56.0 us)
Async XLA Ops:
  0.6 11.5 %copy-start = (f32[256,1024]{1,0:T(8,128)S(1)}, f32[256,1024]{1,0:T(8,128)}, u32[]{:S(2)}) copy-start(f32[256,1024]{1,0:T(8,128)} %param.7) | copy-start | bytes 3145732
  0.6 11.2 %copy-start.24 = (bf16[256,64]{0,1:T(8,128)(2,1)S(1)}, bf16[256,64]{0,1:T(8,128)(2,1)}, u32[]{:S(2)}) copy-start(bf16[256,64]{0,1:T(8,128)(2,1)} %param.4) | copy-start | bytes 98308
  0.7 10.9 %copy-start.27 = (s32[512]{0:T(512)S(1)}, s32[512]{0:T(512)}, u32[]{:S(2)}) copy-start(s32[512]{0:T(512)} %param.5) | copy-start | bytes 6148
  0.7 10.9 %copy-start.26 = (f32[256,16]{0,1:T(8,128)S(1)}, f32[256,16]{0,1:T(8,128)}, u32[]{:S(2)}) copy-start(f32[256,16]{0,1:T(8,128)} %param.6) | copy-start | bytes 49156
  2.4 23.0 %all-to-all-start = ((bf16[16,256,64]{1,2,0:T(8,128)(2,1)}), bf16[16,256,64]{1,2,0:T(8,128)(2,1)S(1)}, u32[]{:S(2)}, u32[]{:S(2)}) async-start(bf16[16,256,64]{1,2,0:T(8,128)(2,1)} %broadcast_in_dim.22), calls=%async_computation | async-start | bytes 1048576 | tf_op jit(solution)/shard_map/all_to_all | solution.py:18
  25.3 1.6 copy-start.22
  54.2 29.1 %all-to-all-start.3 = ((f32[16,72,128]{2,1,0:T(8,128)}), f32[16,72,128]{2,1,0:T(8,128)S(1)}, u32[]{:S(2)}, u32[]{:S(2)}) async-start(f32[16,72,128]{2,1,0:T(8,128)} %broadcast_in_dim.26), calls=%async_computation.3 | async-start | bytes 1179648 | tf_op jit(solution)/shard_map/all_to_all | solution.py:18
  84.1 1.2 copy-start.3
  85.3 1.1 copy-start.6
  86.4 39.3 %copy-start.16 = (f32[16,128]{1,0:T(8,128)S(1)}, f32[16,128]{1,0:T(8,128)}, u32[]{:S(2)}) copy-start(f32[16,128]{1,0:T(8,128)} %slice.39.sums_ref) | copy-start | bytes 24580
  133.5 24.0 %copy-start.1 = (f32[65,256]{1,0:T(8,128)}, f32[65,256]{1,0:T(8,128)S(1)}, u32[]{:S(2)}) copy-start(f32[65,256]{1,0:T(8,128)S(1)} %get-tuple-element.21.own_ref.old_ref) | copy-start | bytes 199684
  134.3 14.4 %all-to-all-start.4 = ((f32[4,65,256]{2,1,0:T(8,128)}), f32[4,65,256]{2,1,0:T(8,128)}, u32[]{:S(2)}, u32[]{:S(2)}) async-start(f32[4,65,256]{2,1,0:T(8,128)} %broadcast_in_dim.29), calls=%async_computation.4 | async-start | bytes 589824 | tf_op jit(solution)/shard_map/all_to_all | solution.py:18
  148.7 1.0 copy-start.10
  149.7 0.9 copy-start.12
  168.1 36.3 %copy-start.2 = (f32[65,256]{1,0:T(8,128)S(1)}, f32[65,256]{1,0:T(8,128)}, u32[]{:S(2)}) copy-start(f32[65,256]{1,0:T(8,128)} %copy-done.1) | copy-start | bytes 199684
  181.4 0.9 copy-start.14
  204.4 0.9 copy-start.8
  214.4 18.6 %copy-start.4 = (f32[65,256]{1,0:T(8,128)}, f32[65,256]{1,0:T(8,128)S(1)}, u32[]{:S(2)}) copy-start(f32[65,256]{1,0:T(8,128)S(1)} %get-tuple-element.27.own_ref) | copy-start | bytes 199684
  215.2 9.3 %all-to-all-start.8 = ((f32[4,65,256]{2,1,0:T(8,128)}), f32[4,65,256]{2,1,0:T(8,128)S(1)}, u32[]{:S(2)}, u32[]{:S(2)}) async-start(f32[4,65,256]{2,1,0:T(8,128)} %broadcast_in_dim.31), calls=%async_computation.8 | async-start | bytes 589824 | tf_op jit(solution)/shard_map/all_to_all | solution.py:18
  224.5 1.0 copy-start.11
  225.5 0.9 copy-start.13
  233.1 15.6 %copy-start.9 = (f32[65,256]{1,0:T(8,128)S(1)}, f32[65,256]{1,0:T(8,128)}, u32[]{:S(2)}) copy-start(f32[65,256]{1,0:T(8,128)} %copy-done.7) | copy-start | bytes 199684
  233.1 9.3 %all-to-all-start.9 = ((f32[4,65,256]{2,1,0:T(8,128)}), f32[4,65,256]{2,1,0:T(8,128)S(1)}, u32[]{:S(2)}, u32[]{:S(2)}) async-start(f32[4,65,256]{2,1,0:T(8,128)} %shard_map.82), calls=%async_computation.9 | async-start | bytes 589824 | tf_op jit(solution)/shard_map/all_to_all | solution.py:605
  244.8 11.2 %all-to-all-start.10 = ((f32[16,8,128]{2,1,0:T(8,128)}), f32[16,8,128]{2,1,0:T(8,128)S(1)}, u32[]{:S(2)}, u32[]{:S(2)}) async-start(f32[16,8,128]{2,1,0:T(8,128)} %get-tuple-element.28), calls=%async_computation.10 | async-start | bytes 131072 | tf_op jit(solution)/shard_map/all_to_all | solution.py:610
  (10 other events, 6.6 us)

commit v3 on v2

--- a/solution.py
+++ b/solution.py
@@ -79,54 +79,79 @@
     return (second * scale, -cross * scale, first * scale)
 
 
-def sweep_four(mat, j, lane, sub):
-    n = mat.shape[0]
-    cols = [jnp.broadcast_to(mat[:, j + q : j + q + 1], mat.shape) for q in range(4)]
-    top = (j // 8) * 8
-
-    def entry(p, q):
-        return jnp.broadcast_to(cols[q][j + p : j + p + 1, :], (8, n))
-
-    p0, p1, p2 = pair_inverse(entry(0, 0), entry(1, 0), entry(1, 1))
-    q00, q01, q10, q11 = entry(2, 0), entry(3, 0), entry(2, 1), entry(3, 1)
+def inverse_four(a):
+    p0, p1, p2 = pair_inverse(a(0, 0), a(1, 0), a(1, 1))
+    q00, q01, q10, q11 = a(2, 0), a(3, 0), a(2, 1), a(3, 1)
     t00, t01 = q00 * p0 + q10 * p1, q00 * p1 + q10 * p2
     t10, t11 = q01 * p0 + q11 * p1, q01 * p1 + q11 * p2
-    w00 = entry(2, 2) - (t00 * q00 + t01 * q10)
-    w01 = entry(3, 2) - (t10 * q00 + t11 * q10)
-    w11 = entry(3, 3) - (t10 * q01 + t11 * q11)
+    w00 = a(2, 2) - (t00 * q00 + t01 * q10)
+    w01 = a(3, 2) - (t10 * q00 + t11 * q10)
+    w11 = a(3, 3) - (t10 * q01 + t11 * q11)
     v0, v1, v2 = pair_inverse(w00, w01, w11)
     s00, s01 = v0 * t00 + v1 * t10, v0 * t01 + v1 * t11
     s10, s11 = v1 * t00 + v2 * t10, v1 * t01 + v2 * t11
     i00 = p0 + (t00 * s00 + t10 * s10)
     i01 = p1 + (t00 * s01 + t10 * s11)
     i11 = p2 + (t01 * s01 + t11 * s11)
-    inv = (
+    return (
         (i00, i01, -s00, -s10),
         (i01, i11, -s01, -s11),
         (-s00, -s01, v0, v1),
         (-s10, -s11, v1, v2),
     )
-    inside = (lane >= j) & (lane < j + 4)
-    rows = [
+
+
+def dot_four(left, right):
+    return (left[0] * right[0] + left[1] * right[1]) + (left[2] * right[2] + left[3] * right[3])
+
+
+def sweep_eight(mat, top, lane, sub):
+    n = mat.shape[0]
+    cols = [jnp.broadcast_to(mat[:, top + q : top + q + 1], mat.shape) for q in range(8)]
+
+    def entry(p, q):
+        p, q = max(p, q), min(p, q)
+        return jnp.broadcast_to(cols[q][top + p : top + p + 1, :], (8, n))
+
+    cross = [[entry(4 + q, k) for q in range(4)] for k in range(4)]
+    first = inverse_four(entry)
+    turn = [[dot_four(first[k], [cross[l][q] for l in range(4)]) for q in range(4)] for k in range(4)]
+
+    def left_over(p, q):
+        return entry(4 + p, 4 + q) - dot_four(
+            [cross[k][p] for k in range(4)], [turn[k][q] for k in range(4)]
+        )
+
+    second = inverse_four(left_over)
+    front = (lane >= top) & (lane < top + 4)
+    back = (lane >= top + 4) & (lane < top + 8)
+    inside = front | back
+    unit = [jnp.where(lane == top + p, 1.0, 0.0) for p in range(8)]
+    rows = [jnp.broadcast_to(mat[top + p : top + p + 1, :], (8, n)) for p in range(8)]
+    ahead = [jnp.where(front, unit[p], rows[p]) for p in range(4)]
+    ahead = [dot_four(first[k], ahead) for k in range(4)]
+    after = [
         jnp.where(
-            inside,
-            jnp.where(lane == j + q, 1.0, 0.0),
-            jnp.broadcast_to(mat[j + q : j + q + 1, :], (8, n)),
-        )
-        for q in range(4)
-    ]
-    pivot_rows = [
-        (inv[p][0] * rows[0] + inv[p][1] * rows[1]) + (inv[p][2] * rows[2] + inv[p][3] * rows[3])
+            back,
+            unit[4 + p],
+            jnp.where(front, 0.0, rows[4 + p]) - dot_four([cross[k][p] for k in range(4)], ahead),
+        )
         for p in range(4)
     ]
+    after = [dot_four(second[p], after) for p in range(4)]
+    ahead = [jnp.where(back, 0.0, ahead[k]) - dot_four(turn[k], after) for k in range(4)]
+    pivot_rows = ahead + after
     tiles = []
     for s in range(0, n, 8):
-        tile = jnp.where(inside, 0.0, mat[s : s + 8])
-        terms = [cols[p][s : s + 8] * pivot_rows[p] for p in range(4)]
-        tile = tile - ((terms[0] + terms[1]) + (terms[2] + terms[3]))
         if s == top:
-            for p in range(4):
-                tile = jnp.where(sub == j - top + p, pivot_rows[p], tile)
+            tile = pivot_rows[0]
+            for p in range(1, 8):
+                tile = jnp.where(sub == p, pivot_rows[p], tile)
+        else:
+            here = [cols[p][s : s + 8] for p in range(8)]
+            tile = jnp.where(inside, 0.0, mat[s : s + 8]) - (
+                dot_four(here[:4], pivot_rows[:4]) + dot_four(here[4:], pivot_rows[4:])
+            )
         tiles.append(tile)
     return jnp.concatenate(tiles, axis=0)
 
@@ -159,32 +184,35 @@
     out_ref[...] = out_ref[...] + jnp.transpose(out_ref[...]) + NOISE * kpp_ref[...]
     lane = lax.broadcasted_iota(jnp.int32, (8, SWEEP), 1)
     sub = lax.broadcasted_iota(jnp.int32, (8, SWEEP), 0)
-    identity = jnp.where(
-        lax.broadcasted_iota(jnp.int32, (SWEEP, SWEEP), 0)
-        == lax.broadcasted_iota(jnp.int32, (SWEEP, SWEEP), 1),
-        1.0,
-        0.0,
-    )
-
-    def block_step(k, carry):
-        here = pl.ds(pl.multiple_of(k * SWEEP, SWEEP), SWEEP)
-        diag = out_ref[here, here]
-        for j in range(0, SWEEP, 4):
-            diag = sweep_four(diag, j, lane, sub)
+
+    def dot(former, latter):
+        return jnp.dot(former, latter, precision=HIGHEST, preferred_element_type=jnp.float32)
+
+    count = size // SWEEP
+    spans = [slice(k * SWEEP, (k + 1) * SWEEP) for k in range(count)]
+    diag = out_ref[spans[0], spans[0]]
+    for k in range(count):
+        for top in range(0, SWEEP, 8):
+            diag = sweep_eight(diag, top, lane, sub)
         diag_ref[...] = diag
-        column = out_ref[:, here]
-        out_ref[here, here] = identity
-        row = jnp.dot(
-            diag_ref[...], out_ref[here, :], precision=HIGHEST, preferred_element_type=jnp.float32
-        )
-        out_ref[:, here] = jnp.zeros((size, SWEEP), jnp.float32)
-        out_ref[...] = out_ref[...] - jnp.dot(
-            column, row, precision=HIGHEST, preferred_element_type=jnp.float32
-        )
-        out_ref[here, :] = row
-        return carry
-
-    lax.fori_loop(0, size // SWEEP, block_step, 0)
+        here = diag_ref[...]
+        row = [here if c == k else dot(here, out_ref[spans[k], spans[c]]) for c in range(count)]
+        if k + 1 < count:
+            ahead = spans[k + 1]
+            diag = out_ref[ahead, ahead] - dot(out_ref[ahead, spans[k]], row[k + 1])
+        for r in range(count):
+            if r == k:
+                continue
+            column = out_ref[spans[r], spans[k]]
+            for c in range(count):
+                if c == k:
+                    out_ref[spans[r], spans[c]] = -dot(column, here)
+                elif r == c == k + 1:
+                    out_ref[spans[r], spans[c]] = diag
+                else:
+                    out_ref[spans[r], spans[c]] = out_ref[spans[r], spans[c]] - dot(column, row[c])
+        for c in range(count):
+            out_ref[spans[k], spans[c]] = row[c]
 
 
 def inverse(turn, bands, kpp):
@@ -326,10 +354,12 @@
 
 def descend_kernel(
     pivots_ref, turned_ref, lead_ref, extra_ref, picks_ref, inv_ref, sums_ref, field_ref, old_ref,
-    gamma_ref, out_ref, new_gamma_ref, coef_ref, columns_ref,
+    gamma_ref, out_ref, copies_ref, new_gamma_ref, coef_ref, columns_ref,
 ):
     features = field_ref.shape[0] - 1
-    lines = sums_ref[...]
+    lines = sums_ref[0]
+    for k in range(1, sums_ref.shape[0]):
+        lines = lines + sums_ref[k]
     low = jnp.concatenate([lines[u : u + 1] for u in range(4)], axis=1)
     full = jnp.concatenate([lines[u : u + 1] for u in range(4, 8)], axis=1)
     coef = jnp.dot(
@@ -363,16 +393,18 @@
 
     each_dimension(pivots_ref, columns_ref, features, 0, body)
     out_ref[...] = (field_ref[...] - out_ref[...]) / NOISE + beta * old_ref[...]
-
-
-def descend(factor, inv, sums, field, old, gamma):
+    copies_ref[...] = jnp.broadcast_to(out_ref[...][None], copies_ref.shape)
+
+
+def descend(factor, inv, sums, field, old, gamma, copies):
     rank, count = factor[2].shape
     return pl.pallas_call(
         descend_kernel,
         in_specs=[VMEM] * 10,
-        out_specs=[VMEM] * 2,
+        out_specs=[VMEM] * 3,
         out_shape=[
             jax.ShapeDtypeStruct(field.shape, jnp.float32),
+            jax.ShapeDtypeStruct((copies,) + field.shape, jnp.float32),
             jax.ShapeDtypeStruct((8, 128), jnp.float32),
         ],
         scratch_shapes=[pltpu.VMEM((16, rank), jnp.bfloat16), pltpu.VMEM((rank, 128), jnp.float32)],
@@ -430,11 +462,10 @@
     ]
     high = total[0:1] + both[0]
     full = total[0:1] + (total[1:2] + total[2:3]) + both[1]
-    for u in range(high.shape[1] // 128):
-        sums_ref[u : 1 + u] = high[:, 128 * u : 128 * u + 128]
-        sums_ref[4 + u : 5 + u] = full[:, 128 * u : 128 * u + 128]
+    lines = [line[:, 128 * u : 128 * u + 128] for line in (high, full) for u in range(4)]
     square = jnp.sum(jnp.sum(field * field, axis=0, keepdims=True), axis=1, keepdims=True)
-    sums_ref[8:16] = jnp.broadcast_to(square, (8, 128))
+    lines = jnp.concatenate(lines + [jnp.broadcast_to(square, (8, 128))], axis=0)
+    sums_ref[...] = jnp.broadcast_to(lines[None], sums_ref.shape)
 
 
 def project(factor, image, field, curve, gamma):
@@ -445,7 +476,7 @@
         out_specs=[VMEM] * 3,
         out_shape=[
             jax.ShapeDtypeStruct(field.shape, jnp.float32),
-            jax.ShapeDtypeStruct((16, 128), jnp.float32),
+            jax.ShapeDtypeStruct((curve.shape[0], 16, 128), jnp.float32),
             jax.ShapeDtypeStruct((8, 128), jnp.float32),
         ],
         scratch_shapes=[pltpu.VMEM((rank, 128), jnp.float32)],
@@ -456,16 +487,17 @@
     )(*factor, image, field, curve, gamma)
 
 
-def image_kernel(fields_ref, row_points_ref, col_points_ref, image_ref):
+def image_kernel(place_ref, fields_ref, points_ref, image_ref):
     blocks, width, count = fields_ref.shape
     features = width - 1
+    high_place, low_place = place_ref[0] // blocks, lax.rem(place_ref[0], blocks)
 
     def dot(former, latter):
         return jnp.dot(former, latter, preferred_element_type=jnp.float32)
 
     sides = []
     for k in range(blocks):
-        points = col_points_ref[k]
+        points = points_ref[k * blocks + low_place]
         spare = jnp.zeros((count, features), jnp.float32)
         wide = jnp.concatenate([points.astype(jnp.float32), spare], axis=1)
         turned_points = jnp.transpose(wide)[0:features]
@@ -483,7 +515,7 @@
         sides.append((with_ones, owned, norms, high, middle, low))
 
     def rows(j, carry):
-        points = row_points_ref[j]
+        points = points_ref[high_place * blocks + j]
         wide = points.astype(jnp.float32)
         own_norms = jnp.sum(wide * wide, axis=1, keepdims=True)
         thrice = jnp.concatenate([points] * 3, axis=1)
@@ -491,7 +523,7 @@
         base = jnp.zeros((count, 2 * features), jnp.float32)
         for k in range(blocks):
             with_ones, owned, norms, high, middle, low = sides[k]
-            dots = dot_nt(points, col_points_ref[k])
+            dots = dot_nt(points, points_ref[k * blocks + low_place])
             kern = jnp.exp(-0.5 * (own_norms + norms - 2.0 * dots))
             cross = dot(thrice, jnp.concatenate([high, middle, low], axis=0))
             weight = kern * (cross + owned)
@@ -511,23 +543,23 @@
         image_ref[j] = jnp.transpose(total)[0:width]
         return carry
 
-    lax.fori_loop(0, row_points_ref.shape[0], rows, 0)
-
-
-def image_part(fields, row_points, col_points):
+    lax.fori_loop(0, blocks, rows, 0)
+
+
+def image_part(place, fields, points):
     blocks, width, count = fields.shape
     return pl.pallas_call(
         image_kernel,
-        in_specs=[VMEM] * 3,
+        in_specs=[pl.BlockSpec(memory_space=pltpu.SMEM), VMEM, VMEM],
         out_specs=VMEM,
-        out_shape=jax.ShapeDtypeStruct((row_points.shape[0], width, count), jnp.float32),
+        out_shape=jax.ShapeDtypeStruct((blocks, width, count), jnp.float32),
         compiler_params=pltpu.CompilerParams(vmem_limit_bytes=24 * 2**20),
         cost_estimate=pl.CostEstimate(
             flops=2 * 5 * blocks * blocks * count * count * 128,
             bytes_accessed=2**20,
             transcendentals=blocks * blocks * count * count,
         ),
-    )(fields, row_points, col_points)
+    )(place, fields, points)
 
 
 def gather_kernel(parts_ref, own_ref, image_ref, curve_ref):
@@ -573,9 +605,6 @@
     by_high = [[high * side + low for high in range(side)] for low in range(side)]
     by_low = [[high * side + low for low in range(side)] for high in range(side)]
     point_blocks = spread(points, "row")
-    grid_blocks = point_blocks.reshape((side, side) + points.shape)
-    row_points = lax.dynamic_index_in_dim(grid_blocks, row // side, 0, keepdims=False)
-    col_points = lax.dynamic_index_in_dim(grid_blocks, row % side, 1, keepdims=False)
     all_points = point_blocks.reshape(-1, features)
     lanes = jnp.arange(samples * features, dtype=jnp.int32)
     picks = (lanes[None, :] == jnp.arange(features, dtype=jnp.int32)[:, None] * samples + col)
@@ -596,14 +625,16 @@
     inv = inverse(col[None], spread(sums[:72], "col"), pivot_block(pivot_data))
 
     gamma = jnp.ones((8, 128), jnp.float32)
-    direction, gamma = descend(
-        factor, inv, sums[72:], residual, jnp.zeros_like(residual), gamma
+    direction, copies, gamma = descend(
+        factor, inv, sums[None, 72:], residual, jnp.zeros_like(residual), gamma, side
     )
     estimate = jnp.zeros_like(residual)
     for iteration in range(ITERS):
-        fields = spread(direction, "row", by_high)
+        fields = lax.all_to_all(
+            copies, "row", 0, 0, axis_index_groups=by_high, tiled=True
+        )
         parts = lax.all_to_all(
-            image_part(fields, row_points, col_points),
+            image_part(row[None], fields, point_blocks),
             "row", 0, 0, axis_index_groups=by_low, tiled=True,
         )
         image, curve = gather_image(parts, direction, row_count)
@@ -611,8 +642,10 @@
         if iteration + 1 < ITERS:
             residual, sums, step = project(factor, image, residual, curve, gamma)
             estimate = step[0, 0] * direction
-            sums = jnp.sum(spread(sums, "row"), axis=0)
-            direction, gamma = descend(factor, inv, sums, residual, direction, gamma)
+            sums = lax.all_to_all(sums, "row", 0, 0, tiled=True)
+            direction, copies, gamma = descend(
+                factor, inv, sums, residual, direction, gamma, side
+            )
     fields = pl.pallas_call(
         advance_kernel,
         in_specs=[VMEM] * 4,

time: 288 us -> 276 us (0.958); the launches traced: 287 us -> 271 us
  Pallas kernels: 89.1 us -> 75.9 us
  waiting for transfers between devices: 37.1 us -> 47.3 us
  blocking collectives: 71.1 us -> 63 us
  local copies, waits for them, and re-layouts: 36.9 us -> 30.3 us
  starting transfers between devices: 38.9 us -> 41.8 us
    all_to_all x3 -> x1, blocking collectives: 28.2 us -> 9.76 us  [spread(): lax.all_to_all(copies, axis, 0, 0, axis_index_groups=groups, tiled=True)]
    pallas_call x1, Pallas kernels: 39.3 us -> 23.3 us  [inverse(): pl.pallas_call(inverse_kernel, out_shape=jax.ShapeDtypeStruct(kpp.shape,...]
    all_to_all x1 -> x3, waiting for transfers between devices: 5.01 us -> 15.8 us  [the longest x2 10.8 us: local(): lax.all_to_all(copies, 'row', 0, 0, axis_index_groups=by_high, tiled=True)]
    all_to_all x1 -> x2, blocking collectives: 8.78 us -> 19.1 us  [the longest x1 10.4 us: local(): sums = lax.all_to_all(sums, 'row', 0, 0, tiled=True)]
    all_to_all x1 -> x3, starting transfers between devices: 3.58 us -> 13.1 us  [the longest x2 9.55 us: local(): lax.all_to_all(copies, 'row', 0, 0, axis_index_groups=by_high, tiled=True)]
    all_to_all x4 -> x3, starting transfers between devices: 31.4 us -> 24.7 us  [spread(): lax.all_to_all(copies, axis, 0, 0, axis_index_groups=groups, tiled=True)]
    dynamic_slice x4 -> x0, local copies, waits for them, and re-layouts: 6.63 us -> none  [the longest x2 3.33 us: local(): lax.dynamic_index_in_dim(grid_blocks, row // side, 0, keepdims=False)]
    unnamed x59 -> x55, local copies, waits for them, and re-layouts: 16 us -> 15.1 us
  transfers between devices with their start and end apart: 6 -> 7, of which waited for: 6 -> 7; matrix products, arithmetic and copies ran while one was open for 7% -> 6% of each run, Pallas kernels for 0% -> 0%
where the time goes in v3:
time: 276 us; the launch traced here: 271 us
  Pallas kernels  75.9 us (28%)
  blocking collectives  63 us (23%)
  waiting for transfers between devices  47.3 us (17%)
  starting transfers between devices  41.8 us (15%)
  local copies, waits for them, and re-layouts  30.3 us (11%)
  matrix products  7.3 us (3%)
  other arithmetic  3.58 us (1%)
    all_to_all x3, waiting for transfers between devices, spread(): lax.all_to_all(copies, axis, 0, 0, axis_index_groups=groups, tiled=True)  26.4 us
    all_to_all x3, starting transfers between devices, spread(): lax.all_to_all(copies, axis, 0, 0, axis_index_groups=groups, tiled=True)  24.7 us
    pallas_call x1, Pallas kernels, inverse(): pl.pallas_call(inverse_kernel, out_shape=jax.ShapeDtypeStruct(kpp.shape,...  23.3 us
    all_to_all x1, blocking collectives, local(): fields = lax.all_to_all(fields, 'col', 0, 0, tiled=True)  21.8 us
    pallas_call x2, Pallas kernels, descend(): pl.pallas_call(descend_kernel, in_specs=[VMEM] * 10, out_specs=[VMEM] * 3...  15.2 us
    unnamed x55, local copies, waits for them, and re-layouts  15.1 us
    pallas_call x2, Pallas kernels, image_part(): pl.pallas_call(image_kernel, in_specs=[pl.BlockSpec(memory_space=pltpu.SM...  13.6 us
    all_to_all x1, blocking collectives, local(): curve = lax.all_to_all(curve, 'row', 0, 0, tiled=True)  12.2 us
  transfers between devices with their start and end apart: 7, of which 7 were waited for; matrix products, arithmetic and copies ran while one was open for 6% of the time, Pallas kernels for 0%

profile of v3, /device:TPU:1, one launch (start us, length us, event | category | flops | bytes accessed | tf_op | source)
XLA Modules:
  0.0 270.6 jit_solution(4251247281335138801)
XLA Ops:
  2.4 9.2 %all-to-all-start = ((bf16[16,256,64]{1,2,0:T(8,128)(2,1)}), bf16[16,256,64]{1,2,0:T(8,128)(2,1)S(1)}, u32[]{:S(2)}, u32[]{:S(2)}) async-start(bf16[16,256,64]{1,2,0:T(8,128)(2,1)} %broadcast_in_dim.19), calls=%async_computation | async-start | bytes 1048576 | tf_op jit(solution)/shard_map/all_to_all | solution.py:18
  13.0 12.4 %all-to-all-done = bf16[16,256,64]{1,2,0:T(8,128)(2,1)S(1)} async-done(((bf16[16,256,64]{1,2,0:T(8,128)(2,1)}), bf16[16,256,64]{1,2,0:T(8,128)(2,1)S(1)}, u32[]{:S(2)}, u32[]{:S(2)}) %all-to-all-start) | async-done | bytes 524320 | tf_op jit(solution)/shard_map/all_to_all | solution.py:18
  27.7 10.5 %shard_map.75 = (f32[512,256]{1,0:T(8,128)S(1)}, f32[512,256]{1,0:T(8,128)S(1)}, f32[88,128]{1,0:T(8,128)S(1)}) custom-call(bf16[512,64]{1,0:T(8,128)(2,1)S(1)} %get-tuple-element.60.pivots_ref, bf16[512,64]{1,0:T(8,128)(2,1)S(1)} %fusion.12.dirs_ref, s32[512,1]{1,0:T(8,128)S(1)} %copy.68.comp_ref, bf16[256,64]{1,0:T(8,128)(2,1)S(1)} %copy.69.points_ref, ...), custom_call_target="tpu_custom_call" | custom-call | flops 817889280 | bytes 4194304 | tf_op jit(solution)/shard_map/pallas_call | solution.py:333
  38.3 9.8 %all_to_all.65 = f32[4,88,128]{2,1,0:T(8,128)S(1)} all-to-all(f32[4,88,128]{2,1,0:T(8,128)S(1)} %broadcast_in_dim.21), channel_id=1, replica_groups={{0,64,128,192},{16,80,144,208},{32,96,160,224},{48,112,176,240},{1,65,1..., dimensions={0} | all-to-all | bytes 360448 | tf_op jit(solution)/shard_map/all_to_all | solution.py:18
  52.1 5.0 %all-to-all-done.2 = f32[4,88,128]{2,1,0:T(8,128)S(1)} async-done(((f32[4,88,128]{2,1,0:T(8,128)}), f32[4,88,128]{2,1,0:T(8,128)S(1)}, u32[]{:S(2)}, u32[]{:S(2)}) %all-to-all-start.2) | async-done | bytes 180256 | tf_op jit(solution)/shard_map/all_to_all | solution.py:18
  58.0 12.1 %all-to-all-start.3 = ((f32[16,72,128]{2,1,0:T(8,128)}), f32[16,72,128]{2,1,0:T(8,128)S(1)}, u32[]{:S(2)}, u32[]{:S(2)}) async-start(f32[16,72,128]{2,1,0:T(8,128)} %broadcast_in_dim.23), calls=%async_computation.3 | async-start | bytes 1179648 | tf_op jit(solution)/shard_map/all_to_all | solution.py:18
  77.7 9.0 %all-to-all-done.3.bands_ref = f32[16,72,128]{2,1,0:T(8,128)S(1)} async-done(((f32[16,72,128]{2,1,0:T(8,128)}), f32[16,72,128]{2,1,0:T(8,128)S(1)}, u32[]{:S(2)}, u32[]{:S(2)}) %all-to-all-start.3) | async-done | bytes 589856 | tf_op jit(solution)/shard_map/all_to_all | solution.py:18
  89.9 23.3 %shard_map.76.inv_ref = f32[512,512]{1,0:T(8,128)S(1)} custom-call(s32[1]{0:T(128)} %bitcast.5.turn_ref, f32[16,72,128]{2,1,0:T(8,128)S(1)} %copy-done.7, f32[512,512]{1,0:T(8,128)S(1)} %copy-done.3), custom_call_target="tpu_custom_call" | custom-call | flops 1000000000 | bytes 3145728 | tf_op jit(solution)/shard_map/pallas_call | solution.py:220
  113.2 7.6 %shard_map.77 = (f32[65,256]{1,0:T(8,128)S(1)}, f32[4,65,256]{2,1,0:T(8,128)S(1)}, f32[8,128]{1,0:T(8,128)S(1)}) custom-call(bf16[512,64]{1,0:T(8,128)(2,1)S(1)} %get-tuple-element.60.pivots_ref, f32[64,256]{1,0:T(8,128)S(1)} %convert_bitcast_fusion.turned_ref, f32[512,256]{1,0:T(8,128)S(1)} %get-tuple-element.20.lead_ref, ...), custom_call_target="tpu_custom_call" | custom-call | flops 272629760 | bytes 5242880 | tf_op jit(solution)/shard_map/pallas_call | solution.py:401
  122.7 6.1 %all-to-all-start.4 = ((f32[4,65,256]{2,1,0:T(8,128)}), f32[4,65,256]{2,1,0:T(8,128)}, u32[]{:S(2)}, u32[]{:S(2)}) async-start(f32[4,65,256]{2,1,0:T(8,128)} %copy-done.10), calls=%async_computation.4 | async-start | bytes 589824 | tf_op jit(solution)/shard_map/all_to_all | solution.py:633
  131.2 6.2 %all-to-all-done.4.fields_ref = f32[4,65,256]{2,1,0:T(8,128)} async-done(((f32[4,65,256]{2,1,0:T(8,128)}), f32[4,65,256]{2,1,0:T(8,128)}, u32[]{:S(2)}, u32[]{:S(2)}) %all-to-all-start.4) | async-done | bytes 266272 | tf_op jit(solution)/shard_map/all_to_all | solution.py:633
  138.6 6.9 %shard_map.78 = f32[4,65,256]{2,1,0:T(8,128)S(1)} custom-call(s32[1]{0:T(128)} %bitcast.place_ref, f32[4,65,256]{2,1,0:T(8,128)} %all-to-all-done.4.fields_ref, bf16[16,256,64]{2,1,0:T(8,128)(2,1)S(1)} %copy-done.1), custom_call_target="tpu_custom_call" | custom-call | flops 1342177280 | bytes 1048576 | tf_op jit(solution)/shard_map/pallas_call | solution.py:551
  145.5 8.8 %all_to_all.66.parts_ref = f32[4,65,256]{2,1,0:T(8,128)} all-to-all(f32[4,65,256]{2,1,0:T(8,128)S(1)} %shard_map.78), channel_id=1, replica_groups={{0,16,32,48},{64,80,96,112},{128,144,160,176},{192,208,224,240},{1,17,3..., dimensions={0} | all-to-all | bytes 532480 | tf_op jit(solution)/shard_map/all_to_all | solution.py:636
  156.1 12.2 %all_to_all.67.curve_ref = f32[16,8,128]{2,1,0:T(8,128)S(1)} all-to-all(f32[16,8,128]{2,1,0:T(8,128)} %get-tuple-element.26), channel_id=1, replica_groups=mesh['row'=16,'col'=16] {'row'}, dimensions={0} | all-to-all | bytes 131072 | tf_op jit(solution)/shard_map/all_to_all | solution.py:641
  169.9 8.0 %shard_map.80 = (f32[65,256]{1,0:T(8,128)S(1)}, f32[16,16,128]{2,1,0:T(8,128)S(1)}, f32[8,128]{1,0:T(8,128)S(1)}) custom-call(bf16[512,64]{1,0:T(8,128)(2,1)S(1)} %get-tuple-element.60.pivots_ref, f32[64,256]{1,0:T(8,128)S(1)} %convert_bitcast_fusion.turned_ref, f32[512,256]{1,0:T(8,128)S(1)} %get-tuple-element.20.lead_ref, ...), custom_call_target="tpu_custom_call" | custom-call | flops 272629760 | bytes 4194304 | tf_op jit(solution)/shard_map/pallas_call | solution.py:473
  178.5 10.4 %all_to_all.68.sums_ref = f32[16,16,128]{2,1,0:T(8,128)S(1)} all-to-all(f32[16,16,128]{2,1,0:T(8,128)S(1)} %get-tuple-element.28), channel_id=1, replica_groups=mesh['row'=16,'col'=16] {'row'}, dimensions={0} | all-to-all | bytes 262144 | tf_op jit(solution)/shard_map/all_to_all | solution.py:645
  188.9 7.6 %shard_map.81 = (f32[65,256]{1,0:T(8,128)S(1)}, f32[4,65,256]{2,1,0:T(8,128)S(1)}, f32[8,128]{1,0:T(8,128)S(1)}) custom-call(bf16[512,64]{1,0:T(8,128)(2,1)S(1)} %get-tuple-element.60.pivots_ref, f32[64,256]{1,0:T(8,128)S(1)} %convert_bitcast_fusion.turned_ref, f32[512,256]{1,0:T(8,128)S(1)} %get-tuple-element.20.lead_ref, ...), custom_call_target="tpu_custom_call" | custom-call | flops 272629760 | bytes 5242880 | tf_op jit(solution)/shard_map/pallas_call | solution.py:401
  203.1 4.7 %all-to-all-done.8.fields_ref = f32[4,65,256]{2,1,0:T(8,128)S(1)} async-done(((f32[4,65,256]{2,1,0:T(8,128)}), f32[4,65,256]{2,1,0:T(8,128)S(1)}, u32[]{:S(2)}, u32[]{:S(2)}) %all-to-all-start.8) | async-done | bytes 266272 | tf_op jit(solution)/shard_map/all_to_all | solution.py:633
  209.0 6.7 %shard_map.82 = f32[4,65,256]{2,1,0:T(8,128)} custom-call(s32[1]{0:T(128)} %bitcast.place_ref, f32[4,65,256]{2,1,0:T(8,128)S(1)} %all-to-all-done.8.fields_ref, bf16[16,256,64]{2,1,0:T(8,128)(2,1)S(1)} %copy-done.2), custom_call_target="tpu_custom_call" | custom-call | flops 1342177280 | bytes 1048576 | tf_op jit(solution)/shard_map/pallas_call | solution.py:551
  215.6 3.6 %all-to-all-start.9 = ((f32[4,65,256]{2,1,0:T(8,128)}), f32[4,65,256]{2,1,0:T(8,128)S(1)}, u32[]{:S(2)}, u32[]{:S(2)}) async-start(f32[4,65,256]{2,1,0:T(8,128)} %shard_map.82), calls=%async_computation.9 | async-start | bytes 589824 | tf_op jit(solution)/shard_map/all_to_all | solution.py:636
  219.9 5.0 %all-to-all-done.9.parts_ref = f32[4,65,256]{2,1,0:T(8,128)S(1)} async-done(((f32[4,65,256]{2,1,0:T(8,128)}), f32[4,65,256]{2,1,0:T(8,128)S(1)}, u32[]{:S(2)}, u32[]{:S(2)}) %all-to-all-start.9) | async-done | bytes 266272 | tf_op jit(solution)/shard_map/all_to_all | solution.py:636
  227.3 4.0 %all-to-all-start.10 = ((f32[16,8,128]{2,1,0:T(8,128)}), f32[16,8,128]{2,1,0:T(8,128)S(1)}, u32[]{:S(2)}, u32[]{:S(2)}) async-start(f32[16,8,128]{2,1,0:T(8,128)} %get-tuple-element.32), calls=%async_computation.10 | async-start | bytes 131072 | tf_op jit(solution)/shard_map/all_to_all | solution.py:641
  233.5 5.0 %all-to-all-done.10.curve_ref = f32[16,8,128]{2,1,0:T(8,128)S(1)} async-done(((f32[16,8,128]{2,1,0:T(8,128)}), f32[16,8,128]{2,1,0:T(8,128)S(1)}, u32[]{:S(2)}, u32[]{:S(2)}) %all-to-all-start.10) | async-done | bytes 65568 | tf_op jit(solution)/shard_map/all_to_all | solution.py:641
  243.0 21.8 %all_to_all.69 = f32[16,1,2080]{2,1,0:T(1,128)S(1)} all-to-all(f32[16,1,2080]{2,1,0:T(1,128)S(1)} %all_to_all.52), channel_id=1, replica_groups=mesh['row'=16,'col'=16] {'col'}, dimensions={0} | all-to-all | bytes 266240 | tf_op jit(solution)/shard_map/all_to_all | solution.py:658
  (103 shorter events, 53.2 us)
Async XLA Ops:
  0.6 11.5 %copy-start = (f32[256,1024]{1,0:T(8,128)S(1)}, f32[256,1024]{1,0:T(8,128)}, u32[]{:S(2)}) copy-start(f32[256,1024]{1,0:T(8,128)} %param.7) | copy-start | bytes 3145732
  0.6 11.2 %copy-start.22 = (bf16[256,64]{0,1:T(8,128)(2,1)S(1)}, bf16[256,64]{0,1:T(8,128)(2,1)}, u32[]{:S(2)}) copy-start(bf16[256,64]{0,1:T(8,128)(2,1)} %param.4) | copy-start | bytes 98308
  0.7 10.9 %copy-start.25 = (s32[512]{0:T(512)S(1)}, s32[512]{0:T(512)}, u32[]{:S(2)}) copy-start(s32[512]{0:T(512)} %param.5) | copy-start | bytes 6148
  0.7 10.9 %copy-start.24 = (f32[256,16]{0,1:T(8,128)S(1)}, f32[256,16]{0,1:T(8,128)}, u32[]{:S(2)}) copy-start(f32[256,16]{0,1:T(8,128)} %param.6) | copy-start | bytes 49156
  2.4 23.0 %all-to-all-start = ((bf16[16,256,64]{1,2,0:T(8,128)(2,1)}), bf16[16,256,64]{1,2,0:T(8,128)(2,1)S(1)}, u32[]{:S(2)}, u32[]{:S(2)}) async-start(bf16[16,256,64]{1,2,0:T(8,128)(2,1)} %broadcast_in_dim.19), calls=%async_computation | async-start | bytes 1048576 | tf_op jit(solution)/shard_map/all_to_all | solution.py:18
  25.3 0.8 copy-start.20
  48.7 8.4 %all-to-all-start.2 = ((f32[4,88,128]{2,1,0:T(8,128)}), f32[4,88,128]{2,1,0:T(8,128)S(1)}, u32[]{:S(2)}, u32[]{:S(2)}) async-start(f32[4,88,128]{2,1,0:T(8,128)} %broadcast_in_dim.22), calls=%async_computation.2 | async-start | bytes 360448 | tf_op jit(solution)/shard_map/all_to_all | solution.py:18
  58.0 28.7 %all-to-all-start.3 = ((f32[16,72,128]{2,1,0:T(8,128)}), f32[16,72,128]{2,1,0:T(8,128)S(1)}, u32[]{:S(2)}, u32[]{:S(2)}) async-start(f32[16,72,128]{2,1,0:T(8,128)} %broadcast_in_dim.23), calls=%async_computation.3 | async-start | bytes 1179648 | tf_op jit(solution)/shard_map/all_to_all | solution.py:18
  86.7 0.8 copy-start.6
  87.6 1.2 copy-start.3
  88.8 1.1 copy-start.7
  122.7 14.7 %all-to-all-start.4 = ((f32[4,65,256]{2,1,0:T(8,128)}), f32[4,65,256]{2,1,0:T(8,128)}, u32[]{:S(2)}, u32[]{:S(2)}) async-start(f32[4,65,256]{2,1,0:T(8,128)} %copy-done.10), calls=%async_computation.4 | async-start | bytes 589824 | tf_op jit(solution)/shard_map/all_to_all | solution.py:633
  137.4 1.2 copy-start.1
  154.3 34.6 %copy-start.5 = (f32[65,256]{1,0:T(8,128)S(1)}, f32[65,256]{1,0:T(8,128)}, u32[]{:S(2)}) copy-start(f32[65,256]{1,0:T(8,128)} %copy-done.4) | copy-start | bytes 199684
  156.0 32.8 %copy-start.17 = (f32[8,128]{1,0:T(8,128)S(1)}, f32[8,128]{1,0:T(8,128)}, u32[]{:S(2)}) copy-start(f32[8,128]{1,0:T(8,128)} %copy-done.15) | copy-start | bytes 12292
  168.3 0.9 copy-start.14
  178.5 18.0 %copy-start.8 = (f32[65,256]{1,0:T(8,128)}, f32[65,256]{1,0:T(8,128)S(1)}, u32[]{:S(2)}) copy-start(f32[65,256]{1,0:T(8,128)S(1)} %get-tuple-element.29.field_ref) | copy-start | bytes 199684
  198.4 9.3 %all-to-all-start.8 = ((f32[4,65,256]{2,1,0:T(8,128)}), f32[4,65,256]{2,1,0:T(8,128)S(1)}, u32[]{:S(2)}, u32[]{:S(2)}) async-start(f32[4,65,256]{2,1,0:T(8,128)} %copy-done.11), calls=%async_computation.8 | async-start | bytes 589824 | tf_op jit(solution)/shard_map/all_to_all | solution.py:633
  207.7 1.2 copy-start.2
  215.6 15.7 %copy-start.9 = (f32[65,256]{1,0:T(8,128)S(1)}, f32[65,256]{1,0:T(8,128)}, u32[]{:S(2)}) copy-start(f32[65,256]{1,0:T(8,128)} %copy-done.8) | copy-start | bytes 199684
  215.6 16.3 %copy-start.13 = (f32[65,256]{1,0:T(8,128)S(1)}, f32[65,256]{1,0:T(8,128)}, u32[]{:S(2)}) copy-start(f32[65,256]{1,0:T(8,128)} %copy-done.12) | copy-start | bytes 199684
  215.6 9.3 %all-to-all-start.9 = ((f32[4,65,256]{2,1,0:T(8,128)}), f32[4,65,256]{2,1,0:T(8,128)S(1)}, u32[]{:S(2)}, u32[]{:S(2)}) async-start(f32[4,65,256]{2,1,0:T(8,128)} %shard_map.82), calls=%async_computation.9 | async-start | bytes 589824 | tf_op jit(solution)/shard_map/all_to_all | solution.py:636
  224.9 0.7 copy-start.21
  227.3 11.2 %all-to-all-start.10 = ((f32[16,8,128]{2,1,0:T(8,128)}), f32[16,8,128]{2,1,0:T(8,128)S(1)}, u32[]{:S(2)}, u32[]{:S(2)}) async-start(f32[16,8,128]{2,1,0:T(8,128)} %get-tuple-element.32), calls=%async_computation.10 | async-start | bytes 131072 | tf_op jit(solution)/shard_map/all_to_all | solution.py:641
  (9 other events, 5.8 us)
